TPU v7x, 32 devices: a whole 2x2x4 slice. The times are simulated.
32 devices in a mesh: section: 8 (over z, core), blk: 4 (over y, x).
Axes of the slice: x: 2, y: 2, z: 4, core: 2. Of those that a mesh axis runs over, the one named last changes fastest.
Arguments:
- held_input: bfloat16 [8, 5120, 128], P('section', 'blk'), may hold values from -6 to 6
- fresh_input: bfloat16 [5120, 128], P('blk'), may hold values from -6 to 6
- stashed: bfloat16 [8, 2, 5120, 128], P('section', None, 'blk'), may hold values from -6 to 6
- held_grad: bfloat16 [8, 5120, 128], P('section', 'blk'), may hold values from -6 to 6
- fresh_grad: bfloat16 [5120, 128], P('blk'), may hold values from -6 to 6
- first_up: bfloat16 [8, 2, 128, 6400], P('section', None, 'blk'), may hold values from -1 to 1
- second_up: bfloat16 [8, 2, 160, 16384], P('section', None, 'blk'), may hold values from -0.5 to 0.5
- first_down: bfloat16 [8, 160, 16384], P('section', 'blk'), may hold values from -0.5 to 0.5
- second_down: bfloat16 [8, 128, 6400], P('section', 'blk'), may hold values from -0.5 to 0.5
Outputs:
- passed_output: bfloat16 [8, 5120, 128], P('section', 'blk')
- passed_grad: bfloat16 [8, 5120, 128], P('section', 'blk')
- grad_first_up: bfloat16 [8, 2, 128, 6400], P('section', None, 'blk')
- grad_second_up: bfloat16 [8, 2, 160, 16384], P('section', None, 'blk')
- grad_first_down: bfloat16 [8, 160, 16384], P('section', 'blk')
- grad_second_down: bfloat16 [8, 128, 6400], P('section', 'blk')
All inputs are finite; a program needn't handle non-finite values.
Results may differ from a plain program's by a relative error of at most 0.0095.
Values may be sent and summed in bfloat16 or wider, within the bound.
A program may use at most 128 MiB of HBM per device.

v0:
```python
import functools
import math

import jax
import jax.numpy as jnp
from jax import lax
from jax.experimental import pallas as pl
from jax.experimental.pallas import tpu as pltpu
from jax.sharding import PartitionSpec as P

FIRST_BLOCKS = 128
FIRST_IN = 40
SECOND_BLOCKS = 160
PAIR = 2
TICKS = 2
JOIN = 8
F32 = jnp.float32
BF16 = jnp.bfloat16


def from_behind(value, axis, by):
    length = lax.axis_size(axis)
    pairs = [(i, i + by) for i in range(length) if 0 <= i + by < length]
    return lax.ppermute(value, axis, pairs)


def partner_of(i, d, n):
    return i ^ d if n & (n - 1) == 0 else (i + d) % n


def send(pieces, n, me):
    arrived = [lax.dynamic_index_in_dim(pieces, me, 0, keepdims=False)]
    for d in range(1, n):
        mine = lax.dynamic_index_in_dim(pieces, partner_of(me, d, n), 0, keepdims=False)
        arrived.append(
            lax.ppermute(mine, "blk", [(i, partner_of(i, d, n)) for i in range(n)])
        )
    return arrived


def total_of(pieces):
    return sum(piece.astype(F32) for piece in pieces)


def wide_of(factor):
    a, width = factor.shape
    block = lax.broadcasted_iota(jnp.int32, (JOIN, width), 0) * FIRST_IN
    column = lax.broadcasted_iota(jnp.int32, (JOIN, width), 1)
    keep = (column >= block) & (column < block + FIRST_IN)
    spread = jnp.broadcast_to(factor.astype(F32)[:, None, :], (a, JOIN, width))
    return jnp.where(keep[None], spread, 0.0).reshape(a * JOIN, width)


def by_r_kernel(factor_ref, values_ref, out_ref):
    a = factor_ref.shape[1]
    t = values_ref.shape[2]
    parts = []
    for i in range(PAIR):
        wide = wide_of(factor_ref[i]).astype(BF16)
        out = jnp.dot(wide, values_ref[i], preferred_element_type=F32)
        parts.append(out.reshape(a, JOIN, t))
    out_ref[...] = jnp.concatenate(parts, axis=1).astype(BF16)


def by_p_kernel(factor_ref, rows_ref, out_ref):
    rows = rows_ref[...].astype(F32)
    a, _, t = rows.shape
    for i in range(PAIR):
        wide = wide_of(factor_ref[i]).astype(BF16)
        mine = rows[:, i * JOIN : (i + 1) * JOIN].reshape(a * JOIN, t).astype(BF16)
        out = lax.dot_general(wide, mine, (((0,), (0,)), ((), ())), preferred_element_type=F32)
        out_ref[i] = out.astype(BF16)


def term_kernel(factor, rows_ref, values_ref, out_ref):
    rows = rows_ref[...].astype(F32)
    a, _, t = rows.shape
    width = values_ref.shape[1]
    block = lax.broadcasted_iota(jnp.int32, (JOIN, width), 0) * FIRST_IN
    column = lax.broadcasted_iota(jnp.int32, (JOIN, width), 1)
    keep = (column >= block) & (column < block + FIRST_IN)
    for i in range(PAIR):
        mine = rows[:, i * JOIN : (i + 1) * JOIN].reshape(a * JOIN, t).astype(BF16)
        full = lax.dot_general(
            mine, values_ref[i], (((1,), (1,)), ((), ())), preferred_element_type=F32
        )
        kept = jnp.where(keep[None], full.reshape(a, JOIN, width), 0.0)
        out_ref[i] = (jnp.sum(kept, axis=1) * factor).astype(BF16)


def call(kernel, flops, out_dims, out_block, out_map, operands, blocks, maps):
    moved = sum(x.size for x in operands) * 2 + math.prod(out_dims) * 2
    return pl.pallas_call(
        kernel,
        grid=(FIRST_BLOCKS // (PAIR * JOIN),),
        in_specs=[pl.BlockSpec(x, m) for x, m in zip(blocks, maps)],
        out_specs=pl.BlockSpec(out_block, out_map),
        out_shape=jax.ShapeDtypeStruct(out_dims, BF16),
        cost_estimate=pl.CostEstimate(flops=flops, bytes_accessed=moved, transcendentals=0),
        compiler_params=pltpu.CompilerParams(vmem_limit_bytes=40 * 1024 * 1024),
    )(*operands)


def lead(i):
    return (i, 0, 0)


def middle_dim(i):
    return (0, i, 0)


def shards(
    held_input,
    fresh_input,
    stashed,
    held_grad,
    fresh_grad,
    first_up,
    second_up,
    first_down,
    second_down,
):
    n = lax.axis_size("blk")
    me = lax.axis_index("blk")
    section_pos = lax.axis_index("section")
    last_section = lax.axis_size("section") - 1
    own_p = FIRST_BLOCKS // n
    own_r = SECOND_BLOCKS // n
    own_groups = own_p // JOIN
    groups = FIRST_BLOCKS // JOIN
    width = JOIN * FIRST_IN
    rows, tokens = held_input.shape[1:]

    def gather(value):
        return lax.all_gather(value, "blk", axis=0, tiled=True)

    up_cut = first_up[0].reshape(2, own_groups, JOIN, FIRST_IN, n, own_r).transpose(4, 1, 0, 5, 2, 3)
    down_cut = second_down[0].reshape(own_groups, JOIN, n, own_r, FIRST_IN).transpose(2, 0, 3, 1, 4)
    cut = jnp.concatenate(
        [
            up_cut.reshape(n, own_groups, 2, own_r, width),
            down_cut.reshape(n, own_groups, 1, own_r, width),
        ],
        axis=2,
    )
    cut = lax.optimization_barrier(cut)
    factors = lax.all_to_all(cut, "blk", split_axis=0, concat_axis=0, tiled=True)
    factors = factors.reshape(groups, 3 * own_r, width)
    up_factor, down_factor = factors[:, : 2 * own_r], factors[:, 2 * own_r :]
    up_second = second_up[0].reshape(2, own_r, FIRST_BLOCKS, -1)
    down_first = first_down[0].reshape(own_r, -1, FIRST_BLOCKS)

    def by_r(factor, values):
        a, t = factor.shape[1], values.shape[1]
        return call(
            by_r_kernel,
            2 * a * FIRST_BLOCKS * width * t,
            (a, FIRST_BLOCKS, t),
            (a, PAIR * JOIN, t),
            middle_dim,
            (factor, values.reshape(groups, width, t)),
            ((PAIR, a, width), (PAIR, width, t)),
            (lead, lead),
        )

    def by_p(factor, values):
        a, _, t = values.shape
        return call(
            by_p_kernel,
            2 * a * FIRST_BLOCKS * width * t,
            (groups, width, t),
            (PAIR, width, t),
            lead,
            (factor, values),
            ((PAIR, a, width), (a, PAIR * JOIN, t)),
            (lead, middle_dim),
        ).reshape(n, rows, t)

    def term_of(values, seen):
        a, _, t = values.shape
        return call(
            functools.partial(term_kernel, factor),
            2 * a * FIRST_BLOCKS * width * t,
            (groups, a, width),
            (PAIR, a, width),
            lead,
            (values, seen.reshape(groups, width, t)),
            ((a, PAIR * JOIN, t), (PAIR, width, t)),
            (middle_dim, lead),
        )

    def middle(values):
        t = values.shape[1]
        spread = by_r(up_factor, values).reshape(2, own_r, FIRST_BLOCKS, t)
        mixed = jnp.einsum("grpo,grpt->grot", up_second, spread, preferred_element_type=F32)
        hidden = (jax.nn.silu(mixed[0]) * mixed[1]).astype(BF16)
        lowered = jnp.einsum("rop,rot->rpt", down_first, hidden, preferred_element_type=F32)
        return spread, mixed, hidden, lowered.astype(BF16)

    def backward(grad_lowered, mixed):
        grad_hidden = jnp.einsum(
            "rop,rpt->rot", down_first, grad_lowered, preferred_element_type=F32
        )
        sg = jax.nn.sigmoid(mixed[0])
        slope = sg * (1.0 + mixed[0] * (1.0 - sg))
        grad_mixed = jnp.stack(
            [grad_hidden * mixed[1] * slope, grad_hidden * mixed[0] * sg]
        ).astype(BF16)
        grad_spread = jnp.einsum(
            "grpo,grot->grpt", up_second, grad_mixed, preferred_element_type=F32
        ).astype(BF16)
        return grad_mixed, grad_spread.reshape(-1, FIRST_BLOCKS, tokens)

    def add(values, added):
        return (values.astype(F32) + added).astype(BF16)

    factor = 1.0 / math.sqrt(TICKS * tokens)
    inputs, grads = held_input[0], held_grad[0]
    inputs_all = gather(inputs)
    grads_all = gather(grads)
    stash_all = gather(jnp.concatenate([stashed[0, k] for k in range(TICKS)], axis=1))
    terms, grads_seen = [], []
    outputs = back = stash = None
    for k in range(TICKS):
        lowered = middle(inputs_all)[3]
        forward_pieces = send(by_p(down_factor, lowered), n, me)
        if stash is None:
            stash_all, _ = lax.optimization_barrier((stash_all, forward_pieces[0]))
            stash = middle(stash_all)
        grad_lowered = by_r(down_factor, grads_all)
        grad_mixed, grad_spread = backward(
            grad_lowered, stash[1][..., k * tokens : (k + 1) * tokens]
        )
        forward_pieces, grad_spread = lax.optimization_barrier((forward_pieces, grad_spread))
        backward_pieces = send(by_p(up_factor, grad_spread), n, me)
        outputs = add(inputs, total_of(forward_pieces))
        terms.append((grad_lowered, grad_mixed, grad_spread))
        grads_seen.append(grads_all)
        if k + 1 < TICKS:
            back = add(grads, total_of(backward_pieces))
            inputs = jnp.where(section_pos == 0, fresh_input, from_behind(outputs, "section", 1))
            grads = jnp.where(
                section_pos == last_section, fresh_grad, from_behind(back, "section", -1)
            )
            inputs_all = gather(inputs)
            grads_all = gather(grads)
    spread, mixed, hidden, lowered = stash
    grad_lowered, grad_mixed, grad_spread = (
        jnp.concatenate([term[i] for term in terms], axis=-1) for i in range(3)
    )
    both = jnp.concatenate(grads_seen, axis=1)

    def finish(total):
        return (total * factor).astype(BF16)

    back_cut = jnp.concatenate([term_of(grad_spread, stash_all), term_of(lowered, both)], axis=1)
    back_cut = back_cut.reshape(n, own_groups, 3, own_r, width)
    small = lax.all_to_all(back_cut, "blk", split_axis=0, concat_axis=0, tiled=True)
    w2 = finish(jnp.einsum("grpt,grot->grpo", spread, grad_mixed, preferred_element_type=F32))
    w3 = finish(jnp.einsum("rot,rpt->rop", hidden, grad_lowered, preferred_element_type=F32))
    back = add(grads, total_of(backward_pieces))
    small = lax.optimization_barrier(small).reshape(n, own_groups, 3, own_r, JOIN, FIRST_IN)
    g1 = small[:, :, :2].transpose(2, 1, 4, 5, 0, 3)
    g4 = small[:, :, 2].transpose(1, 3, 0, 2, 4)
    return (
        outputs.reshape(held_input.shape),
        back.reshape(held_grad.shape),
        g1.reshape(first_up.shape),
        w2.reshape(second_up.shape),
        w3.reshape(first_down.shape),
        g4.reshape(second_down.shape),
    )


def solution(mesh):
    return jax.shard_map(
        shards,
        mesh=mesh,
        in_specs=(
            P("section", "blk", None),
            P("blk", None),
            P("section", None, "blk", None),
            P("section", "blk", None),
            P("blk", None),
            P("section", None, "blk", None),
            P("section", None, "blk", None),
            P("section", "blk", None),
            P("section", "blk", None),
        ),
        out_specs=(
            P("section", "blk", None),
            P("section", "blk", None),
            P("section", None, "blk", None),
            P("section", None, "blk", None),
            P("section", "blk", None),
            P("section", "blk", None),
        ),
        check_vma=False,
    )
```

profile of v0, /device:TPU:16, one launch (start us, length us, event | category | flops | bytes accessed | tf_op | source)
XLA Modules:
  0.0 355.9 jit_solution(10314381718537530941)
XLA Ops:
  10.8 2.4 reshape_squeeze.13
  14.6 8.9 %reshape_squeeze.12 = bf16[2,4,8,40,4,40]{5,4,3,2,1,0:T(4,128)(2,1)S(1)} reshape(bf16[1,2,32,6400]{3,2,1,0:T(8,128)(2,1)} %param.14) | data formatting | bytes 1638400 | tf_op jit(solution)/shard_map/reshape;squeeze | solution.py:137
  23.5 2.5 copy.41
  26.0 2.7 pad_maximum_fusion.2
  28.7 3.7 %all-to-all-start = ((bf16[4,4,3,40,320]{4,3,2,1,0:T(8,128)(2,1)}), bf16[4,4,3,40,320]{4,3,2,1,0:T(8,128)(2,1)S(1)}, u32[]{:S(2)}, u32[]{:S(2)}) async-start(bf16[4,4,3,40,320]{4,3,2,1,0:T(8,128)(2,1)} %pad_maximum_fusion.2), calls=%async_computation | async-start | bytes 2949120 | tf_op jit(solution)/shard_map/all_to_all | solution.py:147
  34.8 2.2 copy.44
  37.1 18.2 %all-to-all-done = bf16[4,4,3,40,320]{4,3,2,1,0:T(8,128)(2,1)S(1)} async-done(((bf16[4,4,3,40,320]{4,3,2,1,0:T(8,128)(2,1)}), bf16[4,4,3,40,320]{4,3,2,1,0:T(8,128)(2,1)S(1)}, u32[]{:S(2)}, u32[]{:S(2)}) %all-to-all-start) | async-done | bytes 1228832 | tf_op jit(solution)/shard_map/all_to_all | solution.py:147
  56.7 3.6 %shard_map.136 = bf16[80,128,128]{2,1,0:T(8,128)(2,1)S(1)} custom-call(bf16[16,80,320]{2,1,0:T(8,128)(2,1)S(1)} %slice.75.factor_ref, bf16[16,320,128]{2,1,0:T(8,128)(2,1)S(1)} %bitcast.277), custom_call_target="tpu_custom_call" | custom-call | flops 838860800 | bytes 4751360 | tf_op jit(solution)/shard_map/pallas_call | solution.py:93
  62.9 3.1 shard_map.137
  70.5 21.6 %all-gather.16.cloned.1.call-done = bf16[1,5120,128]{2,1,0:T(8,128)(2,1)} async-done(((bf16[1,1280,128]{2,1,0:T(8,128)(2,1)}), bf16[1,5120,128]{2,1,0:T(8,128)(2,1)}) %all-gather.16.cloned.1.call-update) | async-done | bytes 1310736 | tf_op jit(solution)/shard_map/all_gather | solution.py:135
  93.4 2.4 shard_map.138
  95.9 38.3 %all-gather.8.cloned.1.call-done = bf16[5120,256]{1,0:T(8,128)(2,1)} async-done(((bf16[1280,256]{1,0:T(8,128)(2,1)}), bf16[5120,256]{1,0:T(8,128)(2,1)}) %all-gather.8.cloned.1.call-update) | async-done | bytes 2621456 | tf_op jit(solution)/shard_map/all_gather | solution.py:135
  135.9 4.4 %shard_map.139 = bf16[80,128,256]{2,1,0:T(8,128)(2,1)S(1)} custom-call(bf16[16,80,320]{2,1,0:T(8,128)(2,1)S(1)} %slice.75.factor_ref, bf16[16,320,256]{2,1,0:T(8,128)(2,1)S(1)} %bitcast.266), custom_call_target="tpu_custom_call" | custom-call | flops 1677721600 | bytes 8683520 | tf_op jit(solution)/shard_map/pallas_call | solution.py:93
  140.4 5.7 %convolution_bitcast_fusion = f32[2,40,128,256]{2,3,1,0:T(8,128)} fusion(bf16[2,40,128,256]{3,2,1,0:T(8,128)(2,1)S(1)} %bitcast.259, bf16[2,40,128,128]{3,2,1,0:T(8,128)(2,1)S(1)} %bitcast.280), kind=kOutput, calls=%fused_computation.14 | convolution fusion | flops 671088640 | bytes 18350080 | tf_op jit(solution)/shard_map/grpo,grpt->grot/dot_general | solution.py:195
  146.1 4.2 %fusion.67 = (bf16[1,40,128,128]{2,3,1,0:T(8,128)(2,1)S(1)}, bf16[1,40,128,128]{2,3,1,0:T(8,128)(2,1)S(1)}) fusion(f32[2,40,128,256]{2,3,1,0:T(8,128)} %convolution_bitcast_fusion, bf16[40,128,128]{2,1,0:T(8,128)(2,1)S(1)} %shard_map.138, bf16[40,128,128]{2,1,0:T(8,128)(2,1)S(1)} %bitcast.292), kind=kOutput, calls=%fused_computation.76 | convolution fusion | flops 176291840 | bytes 10485760 | tf_op jit(solution)/shard_map/rop,rpt->rot/dot_general | solution.py:201
  151.8 3.5 convert_bitcast_fusion.2
  155.3 4.5 %copy.21 = bf16[2,40,128,128]{3,2,1,0:T(8,128)(2,1)} copy(bf16[2,40,128,128]{2,3,1,0:T(8,128)(2,1)} %convert_bitcast_fusion.2) | data formatting | bytes 5242880 | tf_op jit(solution)/shard_map/convert_element_type | solution.py:211
  161.2 1.9 collective-permute-start.3
  163.2 6.5 %collective-permute-done.3 = bf16[1280,128]{1,0:T(8,128)(2,1)S(1)} collective-permute-done((bf16[1280,128]{1,0:T(8,128)(2,1)S(1)}, bf16[1280,128]{1,0:T(8,128)(2,1)S(1)}, u32[]{:S(2)}, u32[]{:S(2)}) %collective-permute-start.3) | collective-permute-done | bytes 327712 | tf_op jit(solution)/shard_map/ppermute | solution.py:24
  172.2 4.3 %shard_map.142 = bf16[16,320,128]{2,1,0:T(8,128)(2,1)S(1)} custom-call(bf16[16,80,320]{2,1,0:T(8,128)(2,1)S(1)} %slice.75.factor_ref, bf16[80,128,128]{2,1,0:T(8,128)(2,1)S(1)} %bitcast.255), custom_call_target="tpu_custom_call" | custom-call | flops 838860800 | bytes 4751360 | tf_op jit(solution)/shard_map/pallas_call | solution.py:93
  180.2 11.6 %collective-permute-done.9 = bf16[1280,128]{1,0:T(8,128)(2,1)S(1)} collective-permute-done((bf16[1280,128]{1,0:T(8,128)(2,1)S(1)}, bf16[1280,128]{1,0:T(8,128)(2,1)S(1)}, u32[]{:S(2)}, u32[]{:S(2)}) %collective-permute-start.9) | collective-permute-done | bytes 327712 | tf_op jit(solution)/shard_map/ppermute | solution.py:36
  191.8 5.1 %collective-permute-done.8 = bf16[1280,128]{1,0:T(8,128)(2,1)S(1)} collective-permute-done((bf16[1280,128]{1,0:T(8,128)(2,1)S(1)}, bf16[1280,128]{1,0:T(8,128)(2,1)S(1)}, u32[]{:S(2)}, u32[]{:S(2)}) %collective-permute-start.8) | collective-permute-done | bytes 327712 | tf_op jit(solution)/shard_map/ppermute | solution.py:36
  197.1 2.3 collective-permute-start.10
  199.4 4.4 %collective-permute-done.10 = bf16[1280,128]{1,0:T(8,128)(2,1)S(1)} collective-permute-done((bf16[1280,128]{1,0:T(8,128)(2,1)S(1)}, bf16[1280,128]{1,0:T(8,128)(2,1)S(1)}, u32[]{:S(2)}, u32[]{:S(2)}) %collective-permute-start.10) | collective-permute-done | bytes 327712 | tf_op jit(solution)/shard_map/ppermute | solution.py:24
  204.5 4.9 %fusion.1 = bf16[40,128,256]{1,2,0:T(8,128)(2,1)S(1)} fusion(f32[2,40,128,256]{2,3,1,0:T(8,128)} %convolution_bitcast_fusion), kind=kLoop, calls=%fused_computation.2 | loop fusion | flops 7864320 | bytes 13107200 | tf_op jit(solution)/shard_map/convert_element_type | solution.py:196
  210.9 2.5 convert_bitcast_fusion.rows_ref
  214.7 3.6 %shard_map.140 = bf16[80,128,128]{2,1,0:T(8,128)(2,1)S(1)} custom-call(bf16[16,80,320]{2,1,0:T(8,128)(2,1)S(1)} %slice.75.factor_ref, bf16[16,320,128]{2,1,0:T(8,128)(2,1)S(1)} %bitcast.278), custom_call_target="tpu_custom_call" | custom-call | flops 838860800 | bytes 4751360 | tf_op jit(solution)/shard_map/pallas_call | solution.py:93
  220.6 3.1 shard_map.141
  228.1 23.2 %all-gather.12.cloned.1.call-done = bf16[5120,128]{1,0:T(8,128)(2,1)} async-done(((bf16[1280,128]{1,0:T(8,128)(2,1)}), bf16[5120,128]{1,0:T(8,128)(2,1)}) %all-gather.12.cloned.1.call-update) | async-done | bytes 1310736 | tf_op jit(solution)/shard_map/all_gather | solution.py:135
  252.6 2.4 shard_map.143
  255.0 4.6 %fusion.68 = (bf16[1,40,128,128]{2,3,1,0:T(8,128)(2,1)S(1)}, bf16[1,40,128,128]{2,3,1,0:T(8,128)(2,1)S(1)}) fusion(f32[2,40,128,256]{2,3,1,0:T(8,128)} %convolution_bitcast_fusion, bf16[40,128,128]{2,1,0:T(8,128)(2,1)S(1)} %shard_map.143, bf16[40,128,128]{2,1,0:T(8,128)(2,1)S(1)} %bitcast.295), kind=kOutput, calls=%fused_computation.77 | convolution fusion | flops 176291840 | bytes 10485760 | tf_op jit(solution)/shard_map/rop,rpt->rot/dot_general | solution.py:201
  261.2 3.5 convert_bitcast_fusion.1
  264.7 4.4 %copy.25 = bf16[2,40,128,128]{3,2,1,0:T(8,128)(2,1)} copy(bf16[2,40,128,128]{2,3,1,0:T(8,128)(2,1)} %convert_bitcast_fusion.1) | data formatting | bytes 5242880 | tf_op jit(solution)/shard_map/convert_element_type | solution.py:211
  271.0 4.3 %shard_map.144 = bf16[16,320,128]{2,1,0:T(8,128)(2,1)S(1)} custom-call(bf16[16,80,320]{2,1,0:T(8,128)(2,1)S(1)} %slice.75.factor_ref, bf16[80,128,128]{2,1,0:T(8,128)(2,1)S(1)} %bitcast.257), custom_call_target="tpu_custom_call" | custom-call | flops 838860800 | bytes 4751360 | tf_op jit(solution)/shard_map/pallas_call | solution.py:93
  277.4 4.5 %multiply_convert_fusion = bf16[2,40,128,128]{3,2,1,0:T(8,128)(2,1)} fusion(bf16[2,40,128,256]{3,2,1,0:T(8,128)(2,1)S(1)} %bitcast.262, bf16[1,40,128,128]{2,3,1,0:T(8,128)(2,1)} %copy-done.37, bf16[1,40,128,128]{2,3,1,0:T(8,128)(2,1)} %copy-done.36, bf16[1,40,128,128]{2,3,1,0:T(8,128)(2,1)S(1)} %copy-done.35, bf16[1,40,128,128]{2,3,1,0:T(8,128)(2,1)S(1)} %copy-done.33), kind=kOutput, calls=%fused_computation.13 | convolution fusion | flops 694681600 | bytes 13107200 | tf_op jit(solution)/shard_map/grpt,grot->grpo/dot_general | solution.py:259
  281.9 2.0 multiply_convert_fusion.1
  288.2 7.4 %shard_map.145 = bf16[16,80,320]{2,1,0:T(8,128)(2,1)S(1)} custom-call(bf16[80,128,256]{2,1,0:T(8,128)(2,1)S(1)} %pad_maximum_fusion.rows_ref, bf16[16,320,256]{2,1,0:T(8,128)(2,1)S(1)} %bitcast.267), custom_call_target="tpu_custom_call" | custom-call | flops 1677721600 | bytes 8683520 | tf_op jit(solution)/shard_map/pallas_call | solution.py:93
  297.4 4.4 %shard_map.146 = bf16[16,40,320]{2,1,0:T(8,128)(2,1)S(1)} custom-call(bf16[40,128,256]{2,1,0:T(8,128)(2,1)S(1)} %copy-done.4, bf16[16,320,256]{2,1,0:T(8,128)(2,1)S(1)} %bitcast.265), custom_call_target="tpu_custom_call" | custom-call | flops 838860800 | bytes 5652480 | tf_op jit(solution)/shard_map/pallas_call | solution.py:93
  303.1 4.3 %all-to-all-start.1 = ((bf16[4,4,3,40,320]{4,3,2,1,0:T(8,128)(2,1)}), bf16[4,4,3,40,320]{4,3,2,1,0:T(8,128)(2,1)}, u32[]{:S(2)}, u32[]{:S(2)}) async-start(bf16[4,4,3,40,320]{4,3,2,1,0:T(8,128)(2,1)} %bitcast.288), calls=%async_computation.1 | async-start | bytes 2949120 | tf_op jit(solution)/shard_map/all_to_all | solution.py:258
  307.5 5.2 %reshape.118 = bf16[1,2,40,16384]{3,2,1,0:T(8,128)(2,1)} reshape(bf16[2,40,128,128]{3,2,1,0:T(8,128)(2,1)} %multiply_convert_fusion) | data formatting | bytes 5242880 | tf_op jit(solution)/shard_map/reshape | solution.py:269
  312.7 3.3 reshape.119
  316.0 2.1 fusion.78
  318.1 1.9 fusion.79
  320.0 5.4 %all-to-all-done.1 = bf16[4,4,3,40,320]{4,3,2,1,0:T(8,128)(2,1)} async-done(((bf16[4,4,3,40,320]{4,3,2,1,0:T(8,128)(2,1)}), bf16[4,4,3,40,320]{4,3,2,1,0:T(8,128)(2,1)}, u32[]{:S(2)}, u32[]{:S(2)}) %all-to-all-start.1) | async-done | bytes 1228832 | tf_op jit(solution)/shard_map/all_to_all | solution.py:258
  325.4 6.4 %reshape.116 = bf16[4,4,3,40,8,40]{5,4,3,2,1,0:T(8,128)(2,1)} reshape(bf16[4,4,3,40,320]{4,3,2,1,0:T(8,128)(2,1)} %all-to-all-done.1) | data formatting | bytes 2457600 | tf_op jit(solution)/shard_map/reshape | solution.py:262
  333.5 4.4 %copy.42 = bf16[4,4,2,40,8,40]{3,0,5,4,1,2:T(4,128)(2,1)} copy(bf16[4,4,2,40,8,40]{5,4,3,2,1,0:T(8,128)(2,1)S(1)} %slice-done.2) | data formatting | bytes 1638400
  337.9 7.6 %reshape.117 = bf16[1,2,32,6400]{3,2,1,0:T(8,128)(2,1)} reshape(bf16[2,4,8,40,4,40]{5,4,3,2,1,0:T(4,128)(2,1)} %bitcast.284) | data formatting | bytes 1638400 | tf_op jit(solution)/shard_map/reshape | solution.py:268
  345.8 3.2 reshape.120
  (148 shorter events, 54.6 us)
Async XLA Ops:
  7.2 3.6 %copy-start.38 = (bf16[1,32,6400]{2,1,0:T(8,128)(2,1)S(1)}, bf16[1,32,6400]{2,1,0:T(8,128)(2,1)}, u32[]{:S(2)}) copy-start(bf16[1,32,6400]{2,1,0:T(8,128)(2,1)} %param.17) | copy-start | bytes 1228804
  7.2 48.2 %all-gather.14.cloned.1.call-start = ((), (), s32[]{:S(2)}) async-start(), calls=%async_computation.5 | async-start | bytes 1638400 | tf_op jit(solution)/shard_map/all_gather | solution.py:135
  7.9 84.2 %all-gather.16.cloned.1.call-start = ((), (), s32[]{:S(2)}) async-start(), calls=%async_computation.6 | async-start | bytes 1638400 | tf_op jit(solution)/shard_map/all_gather | solution.py:135
  8.7 125.5 %all-gather.8.cloned.1.call-start = ((), (), s32[]{:S(2)}) async-start(), calls=%async_computation.2 | async-start | bytes 3276800 | tf_op jit(solution)/shard_map/all_gather | solution.py:135
  26.0 6.6 %copy-start.29 = (bf16[1,40,16384]{2,1,0:T(8,128)(2,1)S(1)}, bf16[1,40,16384]{2,1,0:T(8,128)(2,1)}, u32[]{:S(2)}) copy-start(bf16[1,40,16384]{2,1,0:T(8,128)(2,1)} %param.16) | copy-start | bytes 3932164
  28.7 26.5 %all-to-all-start = ((bf16[4,4,3,40,320]{4,3,2,1,0:T(8,128)(2,1)}), bf16[4,4,3,40,320]{4,3,2,1,0:T(8,128)(2,1)S(1)}, u32[]{:S(2)}, u32[]{:S(2)}) async-start(bf16[4,4,3,40,320]{4,3,2,1,0:T(8,128)(2,1)} %pad_maximum_fusion.2), calls=%async_computation | async-start | bytes 2949120 | tf_op jit(solution)/shard_map/all_to_all | solution.py:147
  32.4 180.9 %all-gather.10.cloned.1.call-start = ((), (), s32[]{:S(2)}) async-start(), calls=%async_computation.3 | async-start | bytes 1638400 | tf_op jit(solution)/shard_map/all_gather | solution.py:135
  32.6 2.2 copy-start.28
  56.7 3.6 %copy-start.17 = (bf16[10,8,128,128]{3,2,1,0:T(8,128)(2,1)S(1)}, bf16[10,8,128,128]{3,2,1,0:T(8,128)(2,1)}, u32[]{:S(2)}) copy-start(bf16[10,8,128,128]{3,2,1,0:T(8,128)(2,1)} %copy.44) | copy-start | bytes 7864324
  67.0 92.8 %collective-permute-start = (bf16[1280,128]{1,0:T(8,128)(2,1)}, bf16[1280,128]{1,0:T(8,128)(2,1)}, u32[]{:S(2)}, u32[]{:S(2)}) collective-permute-start(bf16[1280,128]{1,0:T(8,128)(2,1)} %get-tuple-element.44), channel_id=1, source_target_pairs={{0,1},{1,0},{2,3},{3,2},{4,5},{5,4},{6,7},{7,6},{8,9},{9,8},{10,11... | collective-permute-start | bytes 983048 | tf_op jit(solution)/shard_map/ppermute | solution.py:36
  68.5 91.4 %collective-permute-start.1 = (bf16[1280,128]{1,0:T(8,128)(2,1)}, bf16[1280,128]{1,0:T(8,128)(2,1)}, u32[]{:S(2)}, u32[]{:S(2)}) collective-permute-start(bf16[1280,128]{1,0:T(8,128)(2,1)} %get-tuple-element.43), channel_id=1, source_target_pairs={{0,2},{1,3},{2,0},{3,1},{4,6},{5,7},{6,4},{7,5},{8,10},{9,11},{10,... | collective-permute-start | bytes 983048 | tf_op jit(solution)/shard_map/ppermute | solution.py:36
  69.0 90.8 %collective-permute-start.2 = (bf16[1280,128]{1,0:T(8,128)(2,1)S(1)}, bf16[1280,128]{1,0:T(8,128)(2,1)}, u32[]{:S(2)}, u32[]{:S(2)}) collective-permute-start(bf16[1280,128]{1,0:T(8,128)(2,1)S(1)} %get-tuple-element.42), channel_id=1, source_target_pairs={{0,3},{1,2},{2,1},{3,0},{4,7},{5,6},{6,5},{7,4},{8,11},{9,10},{10,... | collective-permute-start | bytes 983048 | tf_op jit(solution)/shard_map/ppermute | solution.py:36
  95.9 50.2 %copy-start.11 = (bf16[40,128,128]{2,1,0:T(8,128)(2,1)}, bf16[40,128,128]{2,1,0:T(8,128)(2,1)S(1)}, u32[]{:S(2)}) copy-start(bf16[40,128,128]{2,1,0:T(8,128)(2,1)S(1)} %shard_map.138) | copy-start | bytes 3932164
  135.9 4.5 %copy-start.18 = (bf16[10,8,128,128]{3,2,1,0:T(8,128)(2,1)S(1)}, bf16[10,8,128,128]{3,2,1,0:T(8,128)(2,1)}, u32[]{:S(2)}) copy-start(bf16[10,8,128,128]{3,2,1,0:T(8,128)(2,1)} %copy.44) | copy-start | bytes 7864324
  140.4 5.7 %copy-start.3 = (bf16[80,128,256]{2,1,0:T(8,128)(2,1)}, bf16[80,128,256]{2,1,0:T(8,128)(2,1)S(1)}, u32[]{:S(2)}) copy-start(bf16[80,128,256]{2,1,0:T(8,128)(2,1)S(1)} %shard_map.139) | copy-start | bytes 15728644
  140.4 5.7 %copy-start.24 = (bf16[5,8,128,128]{3,2,1,0:T(8,128)(2,1)S(1)}, bf16[5,8,128,128]{3,2,1,0:T(8,128)(2,1)}, u32[]{:S(2)}) copy-start(bf16[5,8,128,128]{3,2,1,0:T(8,128)(2,1)} %copy.45) | copy-start | bytes 3932164
  155.3 4.5 %copy-start.31 = (bf16[1,1280,128]{2,1,0:T(8,128)(2,1)S(1)}, bf16[1,1280,128]{2,1,0:T(8,128)(2,1)}, u32[]{:S(2)}) copy-start(bf16[1,1280,128]{2,1,0:T(8,128)(2,1)} %param.9) | copy-start | bytes 983044
  155.3 14.3 %copy-start.39 = (bf16[1280,128]{1,0:T(8,128)(2,1)S(1)}, bf16[1280,128]{1,0:T(8,128)(2,1)}, u32[]{:S(2)}) copy-start(bf16[1280,128]{1,0:T(8,128)(2,1)} %param.10) | copy-start | bytes 983044
  161.2 8.4 %collective-permute-start.3 = (bf16[1280,128]{1,0:T(8,128)(2,1)S(1)}, bf16[1280,128]{1,0:T(8,128)(2,1)S(1)}, u32[]{:S(2)}, u32[]{:S(2)}) collective-permute-start(bf16[1280,128]{1,0:T(8,128)(2,1)S(1)} %fusion.77), channel_id=1, source_target_pairs={{0,4},{4,8},{8,12},{12,16},{16,20},{20,24},{24,28},{1,5},{5,9},{9,... | collective-permute-start | bytes 983048 | tf_op jit(solution)/shard_map/ppermute | solution.py:24
  170.4 80.9 %all-gather.12.cloned.1.call-start = ((), (), s32[]{:S(2)}) async-start(), calls=%async_computation.4 | async-start | bytes 1638400 | tf_op jit(solution)/shard_map/all_gather | solution.py:135
  172.2 24.7 %copy-start.30 = (bf16[1,1280,128]{2,1,0:T(8,128)(2,1)S(1)}, bf16[1,1280,128]{2,1,0:T(8,128)(2,1)}, u32[]{:S(2)}) copy-start(bf16[1,1280,128]{2,1,0:T(8,128)(2,1)} %param.12) | copy-start | bytes 983044
  176.5 27.2 %copy-start.40 = (bf16[1280,128]{1,0:T(8,128)(2,1)S(1)}, bf16[1280,128]{1,0:T(8,128)(2,1)}, u32[]{:S(2)}) copy-start(bf16[1280,128]{1,0:T(8,128)(2,1)} %param.13) | copy-start | bytes 983044
  176.6 15.2 %collective-permute-start.9 = (bf16[1280,128]{1,0:T(8,128)(2,1)S(1)}, bf16[1280,128]{1,0:T(8,128)(2,1)S(1)}, u32[]{:S(2)}, u32[]{:S(2)}) collective-permute-start(bf16[1280,128]{1,0:T(8,128)(2,1)S(1)} %get-tuple-element.36), channel_id=1, source_target_pairs={{0,3},{1,2},{2,1},{3,0},{4,7},{5,6},{6,5},{7,4},{8,11},{9,10},{10,... | collective-permute-start | bytes 983048 | tf_op jit(solution)/shard_map/ppermute | solution.py:36
  178.2 18.7 %collective-permute-start.8 = (bf16[1280,128]{1,0:T(8,128)(2,1)S(1)}, bf16[1280,128]{1,0:T(8,128)(2,1)S(1)}, u32[]{:S(2)}, u32[]{:S(2)}) collective-permute-start(bf16[1280,128]{1,0:T(8,128)(2,1)S(1)} %get-tuple-element.37), channel_id=1, source_target_pairs={{0,2},{1,3},{2,0},{3,1},{4,6},{5,7},{6,4},{7,5},{8,10},{9,11},{10,... | collective-permute-start | bytes 983048 | tf_op jit(solution)/shard_map/ppermute | solution.py:36
  179.6 17.2 %collective-permute-start.7 = (bf16[1280,128]{1,0:T(8,128)(2,1)S(1)}, bf16[1280,128]{1,0:T(8,128)(2,1)S(1)}, u32[]{:S(2)}, u32[]{:S(2)}) collective-permute-start(bf16[1280,128]{1,0:T(8,128)(2,1)S(1)} %get-tuple-element.35), channel_id=1, source_target_pairs={{0,1},{1,0},{2,3},{3,2},{4,5},{5,4},{6,7},{7,6},{8,9},{9,8},{10,11... | collective-permute-start | bytes 983048 | tf_op jit(solution)/shard_map/ppermute | solution.py:36
  197.1 6.6 %collective-permute-start.10 = (bf16[1280,128]{1,0:T(8,128)(2,1)S(1)}, bf16[1280,128]{1,0:T(8,128)(2,1)S(1)}, u32[]{:S(2)}, u32[]{:S(2)}) collective-permute-start(bf16[1280,128]{1,0:T(8,128)(2,1)S(1)} %fusion.76), channel_id=1, source_target_pairs={{4,0},{8,4},{12,8},{16,12},{20,16},{24,20},{28,24},{5,1},{9,5},{13... | collective-permute-start | bytes 983048 | tf_op jit(solution)/shard_map/ppermute | solution.py:24
  204.5 6.4 %copy-start.25 = (bf16[5,8,128,128]{3,2,1,0:T(8,128)(2,1)S(1)}, bf16[5,8,128,128]{3,2,1,0:T(8,128)(2,1)}, u32[]{:S(2)}) copy-start(bf16[5,8,128,128]{3,2,1,0:T(8,128)(2,1)} %copy.45) | copy-start | bytes 3932164
  214.7 3.6 %copy-start.19 = (bf16[10,8,128,128]{3,2,1,0:T(8,128)(2,1)S(1)}, bf16[10,8,128,128]{3,2,1,0:T(8,128)(2,1)}, u32[]{:S(2)}) copy-start(bf16[10,8,128,128]{3,2,1,0:T(8,128)(2,1)} %copy.44) | copy-start | bytes 7864324
  224.6 44.4 %collective-permute-start.4 = (bf16[1280,128]{1,0:T(8,128)(2,1)}, bf16[1280,128]{1,0:T(8,128)(2,1)}, u32[]{:S(2)}, u32[]{:S(2)}) collective-permute-start(bf16[1280,128]{1,0:T(8,128)(2,1)} %get-tuple-element.40), channel_id=1, source_target_pairs={{0,1},{1,0},{2,3},{3,2},{4,5},{5,4},{6,7},{7,6},{8,9},{9,8},{10,11... | collective-permute-start | bytes 983048 | tf_op jit(solution)/shard_map/ppermute | solution.py:36
  226.1 43.0 %collective-permute-start.5 = (bf16[1280,128]{1,0:T(8,128)(2,1)}, bf16[1280,128]{1,0:T(8,128)(2,1)}, u32[]{:S(2)}, u32[]{:S(2)}) collective-permute-start(bf16[1280,128]{1,0:T(8,128)(2,1)} %get-tuple-element.39), channel_id=1, source_target_pairs={{0,2},{1,3},{2,0},{3,1},{4,6},{5,7},{6,4},{7,5},{8,10},{9,11},{10,... | collective-permute-start | bytes 983048 | tf_op jit(solution)/shard_map/ppermute | solution.py:36
  226.7 42.4 %collective-permute-start.6 = (bf16[1280,128]{1,0:T(8,128)(2,1)S(1)}, bf16[1280,128]{1,0:T(8,128)(2,1)}, u32[]{:S(2)}, u32[]{:S(2)}) collective-permute-start(bf16[1280,128]{1,0:T(8,128)(2,1)S(1)} %get-tuple-element.38), channel_id=1, source_target_pairs={{0,3},{1,2},{2,1},{3,0},{4,7},{5,6},{6,5},{7,4},{8,11},{9,10},{10,... | collective-permute-start | bytes 983048 | tf_op jit(solution)/shard_map/ppermute | solution.py:36
  255.0 4.7 %copy-start.13 = (bf16[40,128,128]{2,1,0:T(8,128)(2,1)}, bf16[40,128,128]{2,1,0:T(8,128)(2,1)S(1)}, u32[]{:S(2)}) copy-start(bf16[40,128,128]{2,1,0:T(8,128)(2,1)S(1)} %shard_map.143) | copy-start | bytes 3932164
  255.0 6.2 %copy-start.20 = (bf16[10,8,128,128]{3,2,1,0:T(8,128)(2,1)S(1)}, bf16[10,8,128,128]{3,2,1,0:T(8,128)(2,1)}, u32[]{:S(2)}) copy-start(bf16[10,8,128,128]{3,2,1,0:T(8,128)(2,1)} %copy.44) | copy-start | bytes 7864324
  269.1 6.2 %copy-start.1 = (bf16[2,40,128,128]{3,2,1,0:T(8,128)(2,1)S(1)}, bf16[2,40,128,128]{3,2,1,0:T(8,128)(2,1)}, u32[]{:S(2)}) copy-start(bf16[2,40,128,128]{3,2,1,0:T(8,128)(2,1)} %copy.21) | copy-start | bytes 7864324
  271.0 5.4 %slice-start = ((s8[5242880]{0:T(1024)(128)(4,1)}), s8[4194304]{0:T(1024)(128)(4,1)S(1)}, s32[]{:S(2)}) async-start(s8[5242880]{0:T(1024)(128)(4,1)} %bitcast.260), calls=%async_computation.7 | async-start | bytes 8388608
  277.3 4.5 %copy-start.12 = (bf16[40,128,128]{2,1,0:T(8,128)(2,1)S(1)}, bf16[40,128,128]{2,1,0:T(8,128)(2,1)}, u32[]{:S(2)}) copy-start(bf16[40,128,128]{2,1,0:T(8,128)(2,1)} %copy-done.11) | copy-start | bytes 3932164
  277.3 4.5 %copy-start.14 = (bf16[40,128,128]{2,1,0:T(8,128)(2,1)S(1)}, bf16[40,128,128]{2,1,0:T(8,128)(2,1)}, u32[]{:S(2)}) copy-start(bf16[40,128,128]{2,1,0:T(8,128)(2,1)} %copy-done.13) | copy-start | bytes 3932164
  277.4 4.5 %copy-start.22 = (bf16[40,128,256]{1,2,0:T(8,128)(2,1)S(1)}, bf16[40,128,256]{1,2,0:T(8,128)(2,1)}, u32[]{:S(2)}) copy-start(bf16[40,128,256]{1,2,0:T(8,128)(2,1)} %copy-done.21) | copy-start | bytes 7864324
  281.9 6.4 %copy-start.6 = (bf16[5120,256]{1,0:T(8,128)(2,1)S(1)}, bf16[5120,256]{1,0:T(8,128)(2,1)}, u32[]{:S(2)}) copy-start(bf16[5120,256]{1,0:T(8,128)(2,1)} %all-gather.8.cloned.1.call-done) | copy-start | bytes 7864324
  284.7 33.4 %collective-permute-start.13 = (bf16[1280,128]{1,0:T(8,128)(2,1)}, bf16[1280,128]{1,0:T(8,128)(2,1)S(1)}, u32[]{:S(2)}, u32[]{:S(2)}) collective-permute-start(bf16[1280,128]{1,0:T(8,128)(2,1)} %get-tuple-element.33), channel_id=1, source_target_pairs={{0,3},{1,2},{2,1},{3,0},{4,7},{5,6},{6,5},{7,4},{8,11},{9,10},{10,... | collective-permute-start | bytes 983048 | tf_op jit(solution)/shard_map/ppermute | solution.py:36
  286.2 31.9 %collective-permute-start.12 = (bf16[1280,128]{1,0:T(8,128)(2,1)}, bf16[1280,128]{1,0:T(8,128)(2,1)S(1)}, u32[]{:S(2)}, u32[]{:S(2)}) collective-permute-start(bf16[1280,128]{1,0:T(8,128)(2,1)} %get-tuple-element.34), channel_id=1, source_target_pairs={{0,2},{1,3},{2,0},{3,1},{4,6},{5,7},{6,4},{7,5},{8,10},{9,11},{10,... | collective-permute-start | bytes 983048 | tf_op jit(solution)/shard_map/ppermute | solution.py:36
  286.8 8.9 %copy-start.8 = (bf16[1,5120,128]{2,1,0:T(8,128)(2,1)S(1)}, bf16[1,5120,128]{2,1,0:T(8,128)(2,1)}, u32[]{:S(2)}) copy-start(bf16[1,5120,128]{2,1,0:T(8,128)(2,1)} %all-gather.16.cloned.1.call-done) | copy-start | bytes 3932164
  286.8 8.9 %copy-start.10 = (bf16[5120,128]{1,0:T(8,128)(2,1)S(1)}, bf16[5120,128]{1,0:T(8,128)(2,1)}, u32[]{:S(2)}) copy-start(bf16[5120,128]{1,0:T(8,128)(2,1)} %all-gather.12.cloned.1.call-done) | copy-start | bytes 3932164
  286.8 31.3 %collective-permute-start.11 = (bf16[1280,128]{1,0:T(8,128)(2,1)S(1)}, bf16[1280,128]{1,0:T(8,128)(2,1)}, u32[]{:S(2)}, u32[]{:S(2)}) collective-permute-start(bf16[1280,128]{1,0:T(8,128)(2,1)S(1)} %get-tuple-element.32), channel_id=1, source_target_pairs={{0,1},{1,0},{2,3},{3,2},{4,5},{5,4},{6,7},{7,6},{8,9},{9,8},{10,11... | collective-permute-start | bytes 983048 | tf_op jit(solution)/shard_map/ppermute | solution.py:36
  303.1 22.3 %all-to-all-start.1 = ((bf16[4,4,3,40,320]{4,3,2,1,0:T(8,128)(2,1)}), bf16[4,4,3,40,320]{4,3,2,1,0:T(8,128)(2,1)}, u32[]{:S(2)}, u32[]{:S(2)}) async-start(bf16[4,4,3,40,320]{4,3,2,1,0:T(8,128)(2,1)} %bitcast.288), calls=%async_computation.1 | async-start | bytes 2949120 | tf_op jit(solution)/shard_map/all_to_all | solution.py:258
  312.7 3.3 copy-start.27
  312.7 5.4 %copy-start.26 = (bf16[1280,128]{1,0:T(8,128)(2,1)S(1)}, bf16[1280,128]{1,0:T(8,128)(2,1)}, u32[]{:S(2)}) copy-start(bf16[1280,128]{1,0:T(8,128)(2,1)} %broadcast_select_fusion) | copy-start | bytes 983044
  337.9 7.6 %slice-start.3 = ((bf16[4,4,3,40,8,40]{5,4,3,2,1,0:T(8,128)(2,1)}), bf16[4,4,1,40,8,40]{5,4,3,2,1,0:T(8,128)(2,1)S(1)}, s32[]{:S(2)}) async-start(bf16[4,4,3,40,8,40]{5,4,3,2,1,0:T(8,128)(2,1)} %reshape.116), calls=%async_computation.10 | async-start | bytes 2621440 | tf_op jit(solution)/shard_map/slice | solution.py:264
  (18 other events, 26.9 us)
Sparse Core Ops, SparseCore 0:
  9.8 42.0 all-gather.13
  53.8 38.2 all-gather.15
  94.5 39.6 all-gather.7
  170.5 36.9 all-gather.9
  209.8 41.4 all-gather.11
where the time goes:
time: 363 us; the launch traced here: 356 us
  waiting for transfers between devices  136 us (37%)
  local copies, waits for them, and re-layouts  82.7 us (23%)
  Pallas kernels  43.1 us (12%)
  matrix products  34.8 us (10%)
  starting transfers between devices  26.6 us (7%)
  other arithmetic  18.2 us (5%)
  between operations  14.9 us (4%)
    all_gather x5, waiting for transfers between devices, gather(): return lax.all_gather(value, 'blk', axis=0, tiled=True)  83.1 us
    pallas_call x11, Pallas kernels, call(): pl.pallas_call(kernel, grid=(FIRST_BLOCKS // (PAIR * JOIN),), in_specs=[p...  43.1 us
    unnamed x90, local copies, waits for them, and re-layouts  27 us
    all_to_all x1, waiting for transfers between devices, shards(): lax.all_to_all(cut, 'blk', split_axis=0, concat_axis=0, tiled=True)  18.2 us
    ppermute x12, waiting for transfers between devices, send(): lax.ppermute(mine, 'blk', [(i, partner_of(i, d, n)) for i in range(n)])  16.7 us
    ppermute x12, starting transfers between devices, send(): lax.ppermute(mine, 'blk', [(i, partner_of(i, d, n)) for i in range(n)])  14 us
    ppermute x2, waiting for transfers between devices, from_behind(): return lax.ppermute(value, axis, pairs)  10.8 us
    convert_element_type x2, local copies, waits for them, and re-layouts, backward(): grad_spread = jnp.einsum('grpo,grot->grpt', up_second, grad_mixed, prefer...  8.94 us
  transfers between devices with their start and end apart: 21, of which 9 were waited for; matrix products, arithmetic and copies ran while one was open for 23% of the time, Pallas kernels for 11%

commit v1 on v0

--- a/solution.py
+++ b/solution.py
@@ -1,4 +1,3 @@
-import functools
 import math
 
 import jax
@@ -18,14 +17,36 @@
 BF16 = jnp.bfloat16
 
 
-def from_behind(value, axis, by):
-    length = lax.axis_size(axis)
-    pairs = [(i, i + by) for i in range(length) if 0 <= i + by < length]
-    return lax.ppermute(value, axis, pairs)
-
-
 def partner_of(i, d, n):
     return i ^ d if n & (n - 1) == 0 else (i + d) % n
+
+
+def source_of(i, d, n):
+    return i ^ d if n & (n - 1) == 0 else (i - d) % n
+
+
+def spread_over(value, n, by):
+    sections = lax.axis_size("section")
+    arrived = []
+    for d in range(n):
+        if d == 0 and by == 0:
+            arrived.append(value)
+            continue
+        pairs = [
+            (s * n + b, (s + by) % sections * n + partner_of(b, d, n))
+            for s in range(sections)
+            for b in range(n)
+        ]
+        arrived.append(lax.ppermute(value, ("section", "blk"), pairs))
+    return arrived
+
+
+def placed(pieces, n, me):
+    rows = pieces[0].shape[0]
+    whole = jnp.zeros((n * rows,) + pieces[0].shape[1:], pieces[0].dtype)
+    for d, piece in enumerate(pieces):
+        whole = lax.dynamic_update_slice_in_dim(whole, piece, source_of(me, d, n) * rows, 0)
+    return whole
 
 
 def send(pieces, n, me):
@@ -72,7 +93,7 @@
         out_ref[i] = out.astype(BF16)
 
 
-def term_kernel(factor, rows_ref, values_ref, out_ref):
+def term_kernel(rows_ref, values_ref, out_ref):
     rows = rows_ref[...].astype(F32)
     a, _, t = rows.shape
     width = values_ref.shape[1]
@@ -85,17 +106,67 @@
             mine, values_ref[i], (((1,), (1,)), ((), ())), preferred_element_type=F32
         )
         kept = jnp.where(keep[None], full.reshape(a, JOIN, width), 0.0)
-        out_ref[i] = (jnp.sum(kept, axis=1) * factor).astype(BF16)
-
-
-def call(kernel, flops, out_dims, out_block, out_map, operands, blocks, maps):
+        out_ref[i] = jnp.sum(kept, axis=1)
+
+
+def cut_kernel(up_ref, down_ref, out_ref, low_ref, high_ref):
+    owners, count, _, own_r, _ = out_ref.shape
+    skip = SECOND_BLOCKS - 128
+    for g in range(2):
+        x = up_ref[g].astype(F32)
+        for i in range(count):
+            for q in range(FIRST_IN):
+                piece = x[i * JOIN : (i + 1) * JOIN, q * SECOND_BLOCKS : (q + 1) * SECOND_BLOCKS]
+                low_ref[pl.ds(q, JOIN, stride=FIRST_IN), :] = piece[:, :128]
+                high_ref[pl.ds(q, JOIN, stride=FIRST_IN), :] = piece[:, skip:]
+            turned = jnp.concatenate([low_ref[...].T, high_ref[...].T[128 - skip :]], axis=0)
+            for o in range(owners):
+                out_ref[o, i, g] = turned[o * own_r : (o + 1) * own_r].astype(BF16)
+    for i in range(count):
+        for o in range(owners):
+            out_ref[o, i, 2] = down_ref[o, i, 0]
+
+
+def join_kernel(cut_ref, out_ref, low_ref, high_ref):
+    owners, count, _, own_r, _ = cut_ref.shape
+    skip = SECOND_BLOCKS - 128
+    for g in range(2):
+        parts = []
+        for i in range(count):
+            x = jnp.concatenate([cut_ref[o, i, g].astype(F32) for o in range(owners)], axis=0)
+            low_ref[...] = x[:128].T
+            high_ref[...] = x[skip:].T
+            pieces = []
+            for q in range(FIRST_IN):
+                pieces.append(low_ref[pl.ds(q, JOIN, stride=FIRST_IN), :])
+                pieces.append(high_ref[pl.ds(q, JOIN, stride=FIRST_IN), :][:, 128 - skip :])
+            parts.append(jnp.concatenate(pieces, axis=1))
+        out_ref[g] = jnp.concatenate(parts, axis=0).astype(BF16)
+
+
+def relay_call(kernel, own_p, out_dims, out_block, out_map, operands, blocks, maps):
+    return pl.pallas_call(
+        kernel,
+        grid=(max(own_p // (PAIR * JOIN), 1),),
+        in_specs=[pl.BlockSpec(x, m) for x, m in zip(blocks, maps)],
+        out_specs=pl.BlockSpec(out_block, out_map),
+        out_shape=jax.ShapeDtypeStruct(out_dims, BF16),
+        scratch_shapes=[pltpu.VMEM((JOIN * FIRST_IN, 128), F32)] * 2,
+        cost_estimate=pl.CostEstimate(
+            flops=0, bytes_accessed=math.prod(out_dims) * 4, transcendentals=0
+        ),
+        compiler_params=pltpu.CompilerParams(vmem_limit_bytes=40 * 1024 * 1024),
+    )(*operands)
+
+
+def call(kernel, flops, out_dims, out_block, out_map, operands, blocks, maps, dtype=BF16):
     moved = sum(x.size for x in operands) * 2 + math.prod(out_dims) * 2
     return pl.pallas_call(
         kernel,
         grid=(FIRST_BLOCKS // (PAIR * JOIN),),
         in_specs=[pl.BlockSpec(x, m) for x, m in zip(blocks, maps)],
         out_specs=pl.BlockSpec(out_block, out_map),
-        out_shape=jax.ShapeDtypeStruct(out_dims, BF16),
+        out_shape=jax.ShapeDtypeStruct(out_dims, dtype),
         cost_estimate=pl.CostEstimate(flops=flops, bytes_accessed=moved, transcendentals=0),
         compiler_params=pltpu.CompilerParams(vmem_limit_bytes=40 * 1024 * 1024),
     )(*operands)
@@ -131,19 +202,21 @@
     width = JOIN * FIRST_IN
     rows, tokens = held_input.shape[1:]
 
-    def gather(value):
-        return lax.all_gather(value, "blk", axis=0, tiled=True)
-
-    up_cut = first_up[0].reshape(2, own_groups, JOIN, FIRST_IN, n, own_r).transpose(4, 1, 0, 5, 2, 3)
+    step = min(PAIR, own_groups)
+    five = lambda i: (0, i, 0, 0, 0)
+    cut_dims = (n, own_groups, 3, own_r, width)
+    cut_block = (n, step, 3, own_r, width)
     down_cut = second_down[0].reshape(own_groups, JOIN, n, own_r, FIRST_IN).transpose(2, 0, 3, 1, 4)
-    cut = jnp.concatenate(
-        [
-            up_cut.reshape(n, own_groups, 2, own_r, width),
-            down_cut.reshape(n, own_groups, 1, own_r, width),
-        ],
-        axis=2,
+    cut = relay_call(
+        cut_kernel,
+        own_p,
+        cut_dims,
+        cut_block,
+        five,
+        (first_up[0], down_cut.reshape(n, own_groups, 1, own_r, width)),
+        ((2, step * JOIN, first_up.shape[3]), (n, step, 1, own_r, width)),
+        (middle_dim, five),
     )
-    cut = lax.optimization_barrier(cut)
     factors = lax.all_to_all(cut, "blk", split_axis=0, concat_axis=0, tiled=True)
     factors = factors.reshape(groups, 3 * own_r, width)
     up_factor, down_factor = factors[:, : 2 * own_r], factors[:, 2 * own_r :]
@@ -179,7 +252,7 @@
     def term_of(values, seen):
         a, _, t = values.shape
         return call(
-            functools.partial(term_kernel, factor),
+            term_kernel,
             2 * a * FIRST_BLOCKS * width * t,
             (groups, a, width),
             (PAIR, a, width),
@@ -187,6 +260,7 @@
             (values, seen.reshape(groups, width, t)),
             ((a, PAIR * JOIN, t), (PAIR, width, t)),
             (middle_dim, lead),
+            F32,
         )
 
     def middle(values):
@@ -215,53 +289,74 @@
         return (values.astype(F32) + added).astype(BF16)
 
     factor = 1.0 / math.sqrt(TICKS * tokens)
+
+    def terms_of(stash, stash_all, grads_all, grad_lowered, grad_mixed, grad_spread):
+        spread, _, hidden, lowered = stash
+        return (
+            term_of(grad_spread, stash_all),
+            term_of(lowered, grads_all),
+            jnp.einsum("grpt,grot->grpo", spread, grad_mixed, preferred_element_type=F32),
+            jnp.einsum("rot,rpt->rop", hidden, grad_lowered, preferred_element_type=F32),
+        )
+
     inputs, grads = held_input[0], held_grad[0]
-    inputs_all = gather(inputs)
-    grads_all = gather(grads)
-    stash_all = gather(jnp.concatenate([stashed[0, k] for k in range(TICKS)], axis=1))
-    terms, grads_seen = [], []
-    outputs = back = stash = None
+    input_pieces = spread_over(inputs, n, 0)
+    grad_pieces = spread_over(grads, n, 0)
+    stash_pieces = [
+        spread_over(lax.optimization_barrier((stashed[0, k], factors[0]))[0], n, 0)
+        for k in range(TICKS)
+    ]
+    totals = stash = None
+    outputs = back = forward_pieces = backward_pieces = None
     for k in range(TICKS):
-        lowered = middle(inputs_all)[3]
+        lowered = middle(placed(input_pieces, n, me))[3]
         forward_pieces = send(by_p(down_factor, lowered), n, me)
-        if stash is None:
-            stash_all, _ = lax.optimization_barrier((stash_all, forward_pieces[0]))
+        if k == 0:
+            stash_pieces[0], _ = lax.optimization_barrier((stash_pieces[0], forward_pieces[0]))
+            stash_all = placed(stash_pieces[0], n, me)
             stash = middle(stash_all)
+            forward_pieces, _ = lax.optimization_barrier((forward_pieces, stash[3]))
+        outputs = add(inputs, total_of(forward_pieces))
+        if k + 1 < TICKS:
+            input_pieces = spread_over(
+                jnp.where(section_pos == last_section, fresh_input, outputs), n, 1
+            )
+        grads_all = placed(grad_pieces, n, me)
         grad_lowered = by_r(down_factor, grads_all)
-        grad_mixed, grad_spread = backward(
-            grad_lowered, stash[1][..., k * tokens : (k + 1) * tokens]
-        )
-        forward_pieces, grad_spread = lax.optimization_barrier((forward_pieces, grad_spread))
+        grad_mixed, grad_spread = backward(grad_lowered, stash[1])
         backward_pieces = send(by_p(up_factor, grad_spread), n, me)
-        outputs = add(inputs, total_of(forward_pieces))
-        terms.append((grad_lowered, grad_mixed, grad_spread))
-        grads_seen.append(grads_all)
         if k + 1 < TICKS:
+            next_pieces, _ = lax.optimization_barrier((stash_pieces[k + 1], backward_pieces[0]))
+            next_all = placed(next_pieces, n, me)
+            next_stash = middle(next_all)
+            input_pieces, backward_pieces, next_stash = lax.optimization_barrier(
+                (input_pieces, backward_pieces, next_stash)
+            )
+            inputs = input_pieces[0]
             back = add(grads, total_of(backward_pieces))
-            inputs = jnp.where(section_pos == 0, fresh_input, from_behind(outputs, "section", 1))
-            grads = jnp.where(
-                section_pos == last_section, fresh_grad, from_behind(back, "section", -1)
-            )
-            inputs_all = gather(inputs)
-            grads_all = gather(grads)
-    spread, mixed, hidden, lowered = stash
-    grad_lowered, grad_mixed, grad_spread = (
-        jnp.concatenate([term[i] for term in terms], axis=-1) for i in range(3)
+            grad_pieces = spread_over(jnp.where(section_pos == 0, fresh_grad, back), n, -1)
+            terms = terms_of(stash, stash_all, grads_all, grad_lowered, grad_mixed, grad_spread)
+            totals = terms if totals is None else [x + y for x, y in zip(totals, terms)]
+            grad_pieces, totals = lax.optimization_barrier((grad_pieces, totals))
+            grads = grad_pieces[0]
+            stash, stash_all = next_stash, next_all
+    terms = terms_of(stash, stash_all, grads_all, grad_lowered, grad_mixed, grad_spread)
+    t1, t4, w2, w3 = (((x + y) * factor).astype(BF16) for x, y in zip(totals, terms))
+    back_cut = jnp.concatenate([t1, t4], axis=1).reshape(cut_dims)
+    small = lax.all_to_all(back_cut, "blk", split_axis=0, concat_axis=0, tiled=True)
+    back = add(grads, total_of(backward_pieces))
+    small = lax.optimization_barrier(small)
+    g1 = relay_call(
+        join_kernel,
+        own_p,
+        first_up.shape[1:],
+        (2, step * JOIN, first_up.shape[3]),
+        middle_dim,
+        (small,),
+        (cut_block,),
+        (five,),
     )
-    both = jnp.concatenate(grads_seen, axis=1)
-
-    def finish(total):
-        return (total * factor).astype(BF16)
-
-    back_cut = jnp.concatenate([term_of(grad_spread, stash_all), term_of(lowered, both)], axis=1)
-    back_cut = back_cut.reshape(n, own_groups, 3, own_r, width)
-    small = lax.all_to_all(back_cut, "blk", split_axis=0, concat_axis=0, tiled=True)
-    w2 = finish(jnp.einsum("grpt,grot->grpo", spread, grad_mixed, preferred_element_type=F32))
-    w3 = finish(jnp.einsum("rot,rpt->rop", hidden, grad_lowered, preferred_element_type=F32))
-    back = add(grads, total_of(backward_pieces))
-    small = lax.optimization_barrier(small).reshape(n, own_groups, 3, own_r, JOIN, FIRST_IN)
-    g1 = small[:, :, :2].transpose(2, 1, 4, 5, 0, 3)
-    g4 = small[:, :, 2].transpose(1, 3, 0, 2, 4)
+    g4 = small[:, :, 2].reshape(n, own_groups, own_r, JOIN, FIRST_IN).transpose(1, 3, 0, 2, 4)
     return (
         outputs.reshape(held_input.shape),
         back.reshape(held_grad.shape),

time: 363 us -> 274 us (0.75)
  the two profiles are of different devices: /device:TPU:16 before, /device:TPU:0 now
where the time goes in v1:
time: 274 us; the launch traced here: 268 us
  local copies, waits for them, and re-layouts  61.2 us (22%)
  Pallas kernels  57.7 us (21%)
  starting transfers between devices  56.8 us (21%)
  waiting for transfers between devices  43.8 us (16%)
  matrix products  33.1 us (12%)
  other arithmetic  14.1 us (5%)
    pallas_call x14, Pallas kernels, call(): pl.pallas_call(kernel, grid=(FIRST_BLOCKS // (PAIR * JOIN),), in_specs=[p...  53.4 us
    ppermute x12, waiting for transfers between devices, send(): lax.ppermute(mine, 'blk', [(i, partner_of(i, d, n)) for i in range(n)])  28.7 us
    ppermute x20, starting transfers between devices, spread_over(): arrived.append(lax.ppermute(value, ('section', 'blk'), pairs))  28.4 us
    ppermute x12, starting transfers between devices, send(): lax.ppermute(mine, 'blk', [(i, partner_of(i, d, n)) for i in range(n)])  20.2 us
    unnamed x80, local copies, waits for them, and re-layouts  18.6 us
    ppermute x20, waiting for transfers between devices, spread_over(): arrived.append(lax.ppermute(value, ('section', 'blk'), pairs))  15.1 us
    dynamic_update_slice x23, local copies, waits for them, and re-layouts, placed(): lax.dynamic_update_slice_in_dim(whole, piece, source_of(me, d, n) * rows, 0)  11.8 us
    dot_general x2, matrix products, terms_of(): jnp.einsum('grpt,grot->grpo', spread, grad_mixed, preferred_element_type=...  9.12 us
  transfers between devices with their start and end apart: 34, of which 7 were waited for; matrix products, arithmetic and copies ran while one was open for 34% of the time, Pallas kernels for 21%

profile of v1, /device:TPU:0, one launch (start us, length us, event | category | flops | bytes accessed | tf_op | source)
XLA Modules:
  0.0 268.5 jit_solution(11234738881378680536)
XLA Ops:
  0.6 3.0 %collective-permute-start = (bf16[1280,128]{1,0:T(8,128)(2,1)}, bf16[1280,128]{1,0:T(8,128)(2,1)}, u32[]{:S(2)}, u32[]{:S(2)}) collective-permute-start(bf16[1280,128]{1,0:T(8,128)(2,1)} %bitcast.330), channel_id=1, source_target_pairs={{0,1},{1,0},{2,3},{3,2},{4,5},{5,4},{6,7},{7,6},{8,9},{9,8},{10,11... | collective-permute-start | bytes 983048 | tf_op jit(solution)/shard_map/ppermute | solution.py:40
  5.2 2.0 collective-permute-start.14
  8.6 3.4 %reshape_squeeze.12 = bf16[4,8,4,40,40]{4,3,2,1,0:T(8,128)(2,1)S(1)} reshape(bf16[1,32,6400]{2,1,0:T(8,128)(2,1)} %param.17) | data formatting | bytes 819200 | tf_op jit(solution)/shard_map/reshape;squeeze | solution.py:209
  13.7 2.2 shard_map.136
  15.9 4.6 %all-to-all-start = ((bf16[4,4,3,40,320]{4,3,2,1,0:T(8,128)(2,1)}), bf16[4,4,3,40,320]{4,3,2,1,0:T(8,128)(2,1)}, u32[]{:S(2)}, u32[]{:S(2)}) async-start(bf16[4,4,3,40,320]{4,3,2,1,0:T(8,128)(2,1)} %shard_map.136), calls=%async_computation | async-start | bytes 2949120 | tf_op jit(solution)/shard_map/all_to_all | solution.py:220
  22.7 2.9 %copy.48 = bf16[5,8,128,128]{3,2,1,0:T(8,128)(2,1)} copy(bf16[5,8,128,128]{3,1,2,0:T(8,128)(2,1)} %bitcast.329) | data formatting | bytes 2621440
  25.6 2.2 copy.47
  27.8 2.9 %collective-permute-start.15 = (bf16[1280,128]{1,0:T(8,128)(2,1)S(1)}, bf16[1280,128]{1,0:T(8,128)(2,1)S(1)}, u32[]{:S(2)}, u32[]{:S(2)}) collective-permute-start(bf16[1280,128]{1,0:T(8,128)(2,1)S(1)} %bitcast.335), channel_id=1, source_target_pairs={{0,3},{1,2},{2,1},{3,0},{4,7},{5,6},{6,5},{7,4},{8,11},{9,10},{10,... | collective-permute-start | bytes 983048 | tf_op jit(solution)/shard_map/ppermute | solution.py:40
  33.8 4.3 %collective-permute-done.14 = bf16[1280,128]{1,0:T(8,128)(2,1)} collective-permute-done((bf16[1280,128]{1,0:T(8,128)(2,1)}, bf16[1280,128]{1,0:T(8,128)(2,1)}, u32[]{:S(2)}, u32[]{:S(2)}) %collective-permute-start.14) | collective-permute-done | bytes 327712 | tf_op jit(solution)/shard_map/ppermute | solution.py:40
  39.1 10.8 %collective-permute-done.15 = bf16[1280,128]{1,0:T(8,128)(2,1)S(1)} collective-permute-done((bf16[1280,128]{1,0:T(8,128)(2,1)S(1)}, bf16[1280,128]{1,0:T(8,128)(2,1)S(1)}, u32[]{:S(2)}, u32[]{:S(2)}) %collective-permute-start.15) | collective-permute-done | bytes 327712 | tf_op jit(solution)/shard_map/ppermute | solution.py:40
  60.8 3.6 %shard_map.137 = bf16[80,128,128]{2,1,0:T(8,128)(2,1)S(1)} custom-call(bf16[16,80,320]{2,1,0:T(8,128)(2,1)S(1)} %slice.72.factor_ref, bf16[16,320,128]{2,1,0:T(8,128)(2,1)S(1)} %bitcast.307), custom_call_target="tpu_custom_call" | custom-call | flops 838860800 | bytes 4751360 | tf_op jit(solution)/shard_map/pallas_call | solution.py:164
  67.0 2.4 shard_map.140
  69.4 3.1 %shard_map.138 = bf16[16,320,128]{2,1,0:T(8,128)(2,1)S(1)} custom-call(bf16[16,40,320]{2,1,0:T(8,128)(2,1)S(1)} %slice.71.factor_ref, bf16[40,128,128]{2,1,0:T(8,128)(2,1)S(1)} %fusion.49.rows_ref), custom_call_target="tpu_custom_call" | custom-call | flops 419430400 | bytes 3031040 | tf_op jit(solution)/shard_map/pallas_call | solution.py:164
  73.0 1.8 collective-permute-start.4
  74.8 7.5 %collective-permute-start.3 = (bf16[1280,128]{1,0:T(8,128)(2,1)S(1)}, bf16[1280,128]{1,0:T(8,128)(2,1)S(1)}, u32[]{:S(2)}, u32[]{:S(2)}) collective-permute-start(bf16[1280,128]{1,0:T(8,128)(2,1)S(1)} %get-tuple-element.91), channel_id=1, source_target_pairs={{0,1},{1,0},{2,3},{3,2},{4,5},{5,4},{6,7},{7,6},{8,9},{9,8},{10,11... | collective-permute-start | bytes 983048 | tf_op jit(solution)/shard_map/ppermute | solution.py:57
  82.7 3.6 %shard_map.139 = bf16[80,128,128]{2,1,0:T(8,128)(2,1)S(1)} custom-call(bf16[16,80,320]{2,1,0:T(8,128)(2,1)S(1)} %slice.72.factor_ref, bf16[16,320,128]{2,1,0:T(8,128)(2,1)S(1)} %bitcast.298), custom_call_target="tpu_custom_call" | custom-call | flops 838860800 | bytes 4751360 | tf_op jit(solution)/shard_map/pallas_call | solution.py:164
  87.4 2.1 fusion.57
  89.5 2.1 fusion.50.rows_ref
  91.6 5.1 %collective-permute-done.4 = bf16[1280,128]{1,0:T(8,128)(2,1)S(1)} collective-permute-done((bf16[1280,128]{1,0:T(8,128)(2,1)S(1)}, bf16[1280,128]{1,0:T(8,128)(2,1)S(1)}, u32[]{:S(2)}, u32[]{:S(2)}) %collective-permute-start.4) | collective-permute-done | bytes 327712 | tf_op jit(solution)/shard_map/ppermute | solution.py:57
  98.8 2.1 collective-permute-start.11
  100.9 3.2 %fusion.48 = f32[2,40,128,128]{3,2,1,0:T(8,128)} fusion(bf16[2,40,128,128]{3,2,1,0:T(8,128)(2,1)S(1)} %bitcast.289, bf16[1,40,128,128]{2,3,1,0:T(8,128)(2,1)S(1)} %get-tuple-element.77, bf16[1,40,128,128]{2,3,1,0:T(8,128)(2,1)S(1)} %get-tuple-element.76), kind=kOutput, calls=%fused_computation.59 | convolution fusion | flops 336855040 | bytes 10485760 | tf_op jit(solution)/shard_map/grpt,grot->grpo/dot_general | solution.py:298
  104.1 3.5 %convert_bitcast_fusion.1 = bf16[2,40,128,128]{2,3,1,0:T(8,128)(2,1)} fusion(bf16[1,40,128,128]{2,3,1,0:T(8,128)(2,1)S(1)} %get-tuple-element.77, bf16[1,40,128,128]{2,3,1,0:T(8,128)(2,1)S(1)} %get-tuple-element.76, bf16[2,40,128,128]{3,2,1,0:T(8,128)(2,1)S(1)} %bitcast.315), kind=kOutput, calls=%fused_computation.50 | convolution fusion | flops 338165760 | bytes 7864320 | tf_op jit(solution)/shard_map/grpo,grot->grpt/dot_general | solution.py:283
  107.6 4.4 %copy.21 = bf16[2,40,128,128]{3,2,1,0:T(8,128)(2,1)} copy(bf16[2,40,128,128]{2,3,1,0:T(8,128)(2,1)} %convert_bitcast_fusion.1) | data formatting | bytes 5242880 | tf_op jit(solution)/shard_map/convert_element_type | solution.py:285
  115.1 5.8 %shard_map.145 = f32[16,80,320]{2,1,0:T(8,128)S(1)} custom-call(bf16[80,128,128]{2,1,0:T(8,128)(2,1)S(1)} %bitcast.292, bf16[16,320,128]{2,1,0:T(8,128)(2,1)S(1)} %bitcast.299), custom_call_target="tpu_custom_call" | custom-call | flops 838860800 | bytes 4751360 | tf_op jit(solution)/shard_map/pallas_call | solution.py:164
  122.2 4.3 %shard_map.141 = bf16[16,320,128]{2,1,0:T(8,128)(2,1)S(1)} custom-call(bf16[16,80,320]{2,1,0:T(8,128)(2,1)S(1)} %slice.72.factor_ref, bf16[80,128,128]{2,1,0:T(8,128)(2,1)S(1)} %bitcast.293), custom_call_target="tpu_custom_call" | custom-call | flops 838860800 | bytes 4751360 | tf_op jit(solution)/shard_map/pallas_call | solution.py:164
  134.7 3.6 %shard_map.142 = bf16[80,128,128]{2,1,0:T(8,128)(2,1)S(1)} custom-call(bf16[16,80,320]{2,1,0:T(8,128)(2,1)S(1)} %slice.72.factor_ref, bf16[16,320,128]{2,1,0:T(8,128)(2,1)S(1)} %bitcast.300), custom_call_target="tpu_custom_call" | custom-call | flops 838860800 | bytes 4751360 | tf_op jit(solution)/shard_map/pallas_call | solution.py:164
  144.9 3.5 %shard_map.146 = f32[16,40,320]{2,1,0:T(8,128)S(1)} custom-call(bf16[40,128,128]{2,1,0:T(8,128)(2,1)S(1)} %copy-done.13, bf16[16,320,128]{2,1,0:T(8,128)(2,1)S(1)} %bitcast.297), custom_call_target="tpu_custom_call" | custom-call | flops 419430400 | bytes 3031040 | tf_op jit(solution)/shard_map/pallas_call | solution.py:164
  149.6 2.8 %collective-permute-done.17 = bf16[1280,128]{1,0:T(8,128)(2,1)S(1)} collective-permute-done((bf16[1280,128]{1,0:T(8,128)(2,1)S(1)}, bf16[1280,128]{1,0:T(8,128)(2,1)S(1)}, u32[]{:S(2)}, u32[]{:S(2)}) %collective-permute-start.17) | collective-permute-done | bytes 327712 | tf_op jit(solution)/shard_map/ppermute | solution.py:57
  154.7 2.7 %collective-permute-start.27 = (bf16[1280,128]{1,0:T(8,128)(2,1)S(1)}, bf16[1280,128]{1,0:T(8,128)(2,1)S(1)}, u32[]{:S(2)}, u32[]{:S(2)}) collective-permute-start(bf16[1280,128]{1,0:T(8,128)(2,1)S(1)} %fusion.68), channel_id=1, source_target_pairs={{0,30},{1,31},{2,28},{3,29},{4,2},{5,3},{6,0},{7,1},{8,6},{9,7},{1... | collective-permute-start | bytes 983048 | tf_op jit(solution)/shard_map/ppermute | solution.py:40
  160.9 4.0 %shard_map.143 = bf16[80,128,128]{2,1,0:T(8,128)(2,1)S(1)} custom-call(bf16[16,80,320]{2,1,0:T(8,128)(2,1)S(1)} %slice.72.factor_ref, bf16[16,320,128]{2,1,0:T(8,128)(2,1)S(1)} %bitcast.308), custom_call_target="tpu_custom_call" | custom-call | flops 838860800 | bytes 4751360 | tf_op jit(solution)/shard_map/pallas_call | solution.py:164
  167.2 3.1 %shard_map.144 = bf16[16,320,128]{2,1,0:T(8,128)(2,1)S(1)} custom-call(bf16[16,40,320]{2,1,0:T(8,128)(2,1)S(1)} %slice.71.factor_ref, bf16[40,128,128]{2,1,0:T(8,128)(2,1)S(1)} %fusion.52.rows_ref), custom_call_target="tpu_custom_call" | custom-call | flops 419430400 | bytes 3031040 | tf_op jit(solution)/shard_map/pallas_call | solution.py:164
  175.8 2.4 shard_map.147
  178.2 3.5 %shard_map.150 = f32[16,40,320]{2,1,0:T(8,128)S(1)} custom-call(bf16[40,128,128]{2,1,0:T(8,128)(2,1)S(1)} %fusion.51.rows_ref, bf16[16,320,128]{2,1,0:T(8,128)(2,1)S(1)} %bitcast.295), custom_call_target="tpu_custom_call" | custom-call | flops 419430400 | bytes 3031040 | tf_op jit(solution)/shard_map/pallas_call | solution.py:164
  181.7 3.1 %fusion.58 = (bf16[1,40,128,128]{2,3,1,0:T(8,128)(2,1)}, bf16[1,40,128,128]{2,3,1,0:T(8,128)(2,1)}) fusion(f32[2,40,128,128]{2,3,1,0:T(8,128)S(1)} %fusion.37, bf16[40,128,128]{2,1,0:T(8,128)(2,1)S(1)} %shard_map.147, bf16[40,128,128]{2,1,0:T(8,128)(2,1)S(1)} %bitcast.324), kind=kOutput, calls=%fused_computation.73 | convolution fusion | flops 176291840 | bytes 10485760 | tf_op jit(solution)/shard_map/rop,rpt->rot/dot_general | solution.py:275
  188.0 5.9 %fusion.47 = f32[2,40,128,128]{3,2,1,0:T(8,128)} fusion(bf16[2,40,128,128]{3,2,1,0:T(8,128)(2,1)} %bitcast.287, bf16[1,40,128,128]{2,3,1,0:T(8,128)(2,1)} %get-tuple-element.75, bf16[1,40,128,128]{2,3,1,0:T(8,128)(2,1)} %get-tuple-element.74), kind=kOutput, calls=%fused_computation.58 | convolution fusion | flops 336855040 | bytes 10485760 | tf_op jit(solution)/shard_map/grpt,grot->grpo/dot_general | solution.py:298
  193.9 3.5 %convert_bitcast_fusion = bf16[2,40,128,128]{2,3,1,0:T(8,128)(2,1)} fusion(bf16[1,40,128,128]{2,3,1,0:T(8,128)(2,1)S(1)} %copy-done.27, bf16[1,40,128,128]{2,3,1,0:T(8,128)(2,1)S(1)} %copy-done.26, bf16[2,40,128,128]{3,2,1,0:T(8,128)(2,1)S(1)} %bitcast.318), kind=kOutput, calls=%fused_computation.49 | convolution fusion | flops 338165760 | bytes 7864320 | tf_op jit(solution)/shard_map/grpo,grot->grpt/dot_general | solution.py:283
  197.4 4.4 %copy.29 = bf16[2,40,128,128]{3,2,1,0:T(8,128)(2,1)} copy(bf16[2,40,128,128]{2,3,1,0:T(8,128)(2,1)} %convert_bitcast_fusion) | data formatting | bytes 5242880 | tf_op jit(solution)/shard_map/convert_element_type | solution.py:285
  201.8 6.7 %multiply_convert_fusion = bf16[2,40,128,128]{3,2,1,0:T(8,128)(2,1)} fusion(f32[2,40,128,128]{3,2,1,0:T(8,128)} %fusion.48, f32[2,40,128,128]{3,2,1,0:T(8,128)} %fusion.47), kind=kLoop, calls=%fused_computation | loop fusion | flops 3932160 | bytes 13107200 | tf_op jit(solution)/shard_map/convert_element_type | solution.py:344
  208.5 5.3 %reshape.117 = bf16[1,2,40,16384]{3,2,1,0:T(8,128)(2,1)} reshape(bf16[2,40,128,128]{3,2,1,0:T(8,128)(2,1)} %multiply_convert_fusion) | data formatting | bytes 5242880 | tf_op jit(solution)/shard_map/reshape | solution.py:364
  215.6 5.9 %shard_map.149 = f32[16,80,320]{2,1,0:T(8,128)S(1)} custom-call(bf16[80,128,128]{2,1,0:T(8,128)(2,1)S(1)} %bitcast.290, bf16[16,320,128]{2,1,0:T(8,128)(2,1)S(1)} %bitcast.301), custom_call_target="tpu_custom_call" | custom-call | flops 838860800 | bytes 4751360 | tf_op jit(solution)/shard_map/pallas_call | solution.py:164
  224.7 3.6 %all-to-all-start.1 = ((bf16[4,4,3,40,320]{4,3,2,1,0:T(8,128)(2,1)}), bf16[4,4,3,40,320]{4,3,2,1,0:T(8,128)(2,1)S(1)}, u32[]{:S(2)}, u32[]{:S(2)}) async-start(bf16[4,4,3,40,320]{4,3,2,1,0:T(8,128)(2,1)} %bitcast.325), calls=%async_computation.1 | async-start | bytes 2949120 | tf_op jit(solution)/shard_map/all_to_all | solution.py:346
  230.0 4.3 %shard_map.148 = bf16[16,320,128]{2,1,0:T(8,128)(2,1)S(1)} custom-call(bf16[16,80,320]{2,1,0:T(8,128)(2,1)S(1)} %slice.72.factor_ref, bf16[80,128,128]{2,1,0:T(8,128)(2,1)S(1)} %bitcast.291), custom_call_target="tpu_custom_call" | custom-call | flops 838860800 | bytes 4751360 | tf_op jit(solution)/shard_map/pallas_call | solution.py:164
  234.4 2.1 collective-permute-start.29
  238.0 2.2 fusion.69
  240.3 14.6 %collective-permute-done.29 = bf16[1280,128]{1,0:T(8,128)(2,1)S(1)} collective-permute-done((bf16[1280,128]{1,0:T(8,128)(2,1)S(1)}, bf16[1280,128]{1,0:T(8,128)(2,1)S(1)}, u32[]{:S(2)}, u32[]{:S(2)}) %collective-permute-start.29) | collective-permute-done | bytes 327712 | tf_op jit(solution)/shard_map/ppermute | solution.py:57
  254.9 5.8 %collective-permute-done.31 = bf16[1280,128]{1,0:T(8,128)(2,1)S(1)} collective-permute-done((bf16[1280,128]{1,0:T(8,128)(2,1)S(1)}, bf16[1280,128]{1,0:T(8,128)(2,1)S(1)}, u32[]{:S(2)}, u32[]{:S(2)}) %collective-permute-start.31) | collective-permute-done | bytes 327712 | tf_op jit(solution)/shard_map/ppermute | solution.py:57
  261.7 2.1 shard_map.151
  265.1 3.2 %reshape.119 = bf16[1,32,6400]{2,1,0:T(8,128)(2,1)} reshape(bf16[4,8,4,40,40]{4,3,2,1,0:T(8,128)(2,1)S(1)} %copy.32) | data formatting | bytes 819200 | tf_op jit(solution)/shard_map/reshape | solution.py:366
  (189 shorter events, 75.5 us)
Async XLA Ops:
  0.6 27.2 %collective-permute-start = (bf16[1280,128]{1,0:T(8,128)(2,1)}, bf16[1280,128]{1,0:T(8,128)(2,1)}, u32[]{:S(2)}, u32[]{:S(2)}) collective-permute-start(bf16[1280,128]{1,0:T(8,128)(2,1)} %bitcast.330), channel_id=1, source_target_pairs={{0,1},{1,0},{2,3},{3,2},{4,5},{5,4},{6,7},{7,6},{8,9},{9,8},{10,11... | collective-permute-start | bytes 983048 | tf_op jit(solution)/shard_map/ppermute | solution.py:40
  3.6 35.4 %collective-permute-start.2 = (bf16[1280,128]{1,0:T(8,128)(2,1)}, bf16[1280,128]{1,0:T(8,128)(2,1)}, u32[]{:S(2)}, u32[]{:S(2)}) collective-permute-start(bf16[1280,128]{1,0:T(8,128)(2,1)} %bitcast.331), channel_id=1, source_target_pairs={{0,3},{1,2},{2,1},{3,0},{4,7},{5,6},{6,5},{7,4},{8,11},{9,10},{10,... | collective-permute-start | bytes 983048 | tf_op jit(solution)/shard_map/ppermute | solution.py:40
  5.1 27.6 %collective-permute-start.1 = (bf16[1280,128]{1,0:T(8,128)(2,1)}, bf16[1280,128]{1,0:T(8,128)(2,1)}, u32[]{:S(2)}, u32[]{:S(2)}) collective-permute-start(bf16[1280,128]{1,0:T(8,128)(2,1)} %bitcast.332), channel_id=1, source_target_pairs={{0,2},{1,3},{2,0},{3,1},{4,6},{5,7},{6,4},{7,5},{8,10},{9,11},{10,... | collective-permute-start | bytes 983048 | tf_op jit(solution)/shard_map/ppermute | solution.py:40
  5.2 32.9 %collective-permute-start.14 = (bf16[1280,128]{1,0:T(8,128)(2,1)}, bf16[1280,128]{1,0:T(8,128)(2,1)}, u32[]{:S(2)}, u32[]{:S(2)}) collective-permute-start(bf16[1280,128]{1,0:T(8,128)(2,1)} %bitcast.333), channel_id=1, source_target_pairs={{0,2},{1,3},{2,0},{3,1},{4,6},{5,7},{6,4},{7,5},{8,10},{9,11},{10,... | collective-permute-start | bytes 983048 | tf_op jit(solution)/shard_map/ppermute | solution.py:40
  7.2 24.6 %collective-permute-start.13 = (bf16[1280,128]{1,0:T(8,128)(2,1)}, bf16[1280,128]{1,0:T(8,128)(2,1)}, u32[]{:S(2)}, u32[]{:S(2)}) collective-permute-start(bf16[1280,128]{1,0:T(8,128)(2,1)} %bitcast.334), channel_id=1, source_target_pairs={{0,1},{1,0},{2,3},{3,2},{4,5},{5,4},{6,7},{7,6},{8,9},{9,8},{10,11... | collective-permute-start | bytes 983048 | tf_op jit(solution)/shard_map/ppermute | solution.py:40
  15.9 4.7 %copy-start.36 = (bf16[1,2,1280,128]{3,2,1,0:T(8,128)(2,1)S(1)}, bf16[1,2,1280,128]{3,2,1,0:T(8,128)(2,1)}, u32[]{:S(2)}) copy-start(bf16[1,2,1280,128]{3,2,1,0:T(8,128)(2,1)} %param.11) | copy-start | bytes 1966084
  15.9 36.1 %all-to-all-start = ((bf16[4,4,3,40,320]{4,3,2,1,0:T(8,128)(2,1)}), bf16[4,4,3,40,320]{4,3,2,1,0:T(8,128)(2,1)}, u32[]{:S(2)}, u32[]{:S(2)}) async-start(bf16[4,4,3,40,320]{4,3,2,1,0:T(8,128)(2,1)} %shard_map.136), calls=%async_computation | async-start | bytes 2949120 | tf_op jit(solution)/shard_map/all_to_all | solution.py:220
  27.8 22.0 %collective-permute-start.15 = (bf16[1280,128]{1,0:T(8,128)(2,1)S(1)}, bf16[1280,128]{1,0:T(8,128)(2,1)S(1)}, u32[]{:S(2)}, u32[]{:S(2)}) collective-permute-start(bf16[1280,128]{1,0:T(8,128)(2,1)S(1)} %bitcast.335), channel_id=1, source_target_pairs={{0,3},{1,2},{2,1},{3,0},{4,7},{5,6},{6,5},{7,4},{8,11},{9,10},{10,... | collective-permute-start | bytes 983048 | tf_op jit(solution)/shard_map/ppermute | solution.py:40
  52.0 20.7 %collective-permute-start.8 = (bf16[1280,128]{1,0:T(8,128)(2,1)}, bf16[1280,128]{1,0:T(8,128)(2,1)S(1)}, u32[]{:S(2)}, u32[]{:S(2)}) collective-permute-start(bf16[1280,128]{1,0:T(8,128)(2,1)} %get-tuple-element.41), channel_id=1, source_target_pairs={{0,3},{1,2},{2,1},{3,0},{4,7},{5,6},{6,5},{7,4},{8,11},{9,10},{10,... | collective-permute-start | bytes 983048 | tf_op jit(solution)/shard_map/ppermute | solution.py:40
  53.3 19.7 %collective-permute-start.7 = (bf16[1280,128]{1,0:T(8,128)(2,1)}, bf16[1280,128]{1,0:T(8,128)(2,1)S(1)}, u32[]{:S(2)}, u32[]{:S(2)}) collective-permute-start(bf16[1280,128]{1,0:T(8,128)(2,1)} %get-tuple-element.41), channel_id=1, source_target_pairs={{0,2},{1,3},{2,0},{3,1},{4,6},{5,7},{6,4},{7,5},{8,10},{9,11},{10,... | collective-permute-start | bytes 983048 | tf_op jit(solution)/shard_map/ppermute | solution.py:40
  54.9 19.9 %collective-permute-start.6 = (bf16[1280,128]{1,0:T(8,128)(2,1)}, bf16[1280,128]{1,0:T(8,128)(2,1)S(1)}, u32[]{:S(2)}, u32[]{:S(2)}) collective-permute-start(bf16[1280,128]{1,0:T(8,128)(2,1)} %get-tuple-element.41), channel_id=1, source_target_pairs={{0,1},{1,0},{2,3},{3,2},{4,5},{5,4},{6,7},{7,6},{8,9},{9,8},{10,11... | collective-permute-start | bytes 983048 | tf_op jit(solution)/shard_map/ppermute | solution.py:40
  55.4 5.3 %copy-start.15 = (bf16[5120,128]{1,0:T(8,128)(2,1)S(1)}, bf16[5120,128]{1,0:T(8,128)(2,1)}, u32[]{:S(2)}) copy-start(bf16[5120,128]{1,0:T(8,128)(2,1)} %copy-done.14) | copy-start | bytes 3932164
  55.4 71.1 %collective-permute-start.21 = (bf16[1280,128]{1,0:T(8,128)(2,1)}, bf16[1280,128]{1,0:T(8,128)(2,1)}, u32[]{:S(2)}, u32[]{:S(2)}) collective-permute-start(bf16[1280,128]{1,0:T(8,128)(2,1)} %get-tuple-element.50), channel_id=1, source_target_pairs={{0,3},{1,2},{2,1},{3,0},{4,7},{5,6},{6,5},{7,4},{8,11},{9,10},{10,... | collective-permute-start | bytes 983048 | tf_op jit(solution)/shard_map/ppermute | solution.py:40
  56.8 70.8 %collective-permute-start.20 = (bf16[1280,128]{1,0:T(8,128)(2,1)}, bf16[1280,128]{1,0:T(8,128)(2,1)}, u32[]{:S(2)}, u32[]{:S(2)}) collective-permute-start(bf16[1280,128]{1,0:T(8,128)(2,1)} %get-tuple-element.50), channel_id=1, source_target_pairs={{0,2},{1,3},{2,0},{3,1},{4,6},{5,7},{6,4},{7,5},{8,10},{9,11},{10,... | collective-permute-start | bytes 983048 | tf_op jit(solution)/shard_map/ppermute | solution.py:40
  69.4 18.0 %copy-start.10 = (bf16[40,128,128]{2,1,0:T(8,128)(2,1)}, bf16[40,128,128]{2,1,0:T(8,128)(2,1)S(1)}, u32[]{:S(2)}) copy-start(bf16[40,128,128]{2,1,0:T(8,128)(2,1)S(1)} %shard_map.140) | copy-start | bytes 3932164
  72.6 9.8 %copy-start.31 = (bf16[1280,128]{1,0:T(8,128)(2,1)S(1)}, bf16[1280,128]{1,0:T(8,128)(2,1)}, u32[]{:S(2)}) copy-start(bf16[1280,128]{1,0:T(8,128)(2,1)} %get-tuple-element.41) | copy-start | bytes 983044
  72.7 18.9 %collective-permute-start.5 = (bf16[1280,128]{1,0:T(8,128)(2,1)S(1)}, bf16[1280,128]{1,0:T(8,128)(2,1)S(1)}, u32[]{:S(2)}, u32[]{:S(2)}) collective-permute-start(bf16[1280,128]{1,0:T(8,128)(2,1)S(1)} %get-tuple-element.89), channel_id=1, source_target_pairs={{0,3},{1,2},{2,1},{3,0},{4,7},{5,6},{6,5},{7,4},{8,11},{9,10},{10,... | collective-permute-start | bytes 983048 | tf_op jit(solution)/shard_map/ppermute | solution.py:57
  73.0 23.7 %collective-permute-start.4 = (bf16[1280,128]{1,0:T(8,128)(2,1)S(1)}, bf16[1280,128]{1,0:T(8,128)(2,1)S(1)}, u32[]{:S(2)}, u32[]{:S(2)}) collective-permute-start(bf16[1280,128]{1,0:T(8,128)(2,1)S(1)} %get-tuple-element.90), channel_id=1, source_target_pairs={{0,2},{1,3},{2,0},{3,1},{4,6},{5,7},{6,4},{7,5},{8,10},{9,11},{10,... | collective-permute-start | bytes 983048 | tf_op jit(solution)/shard_map/ppermute | solution.py:57
  74.8 21.9 %collective-permute-start.3 = (bf16[1280,128]{1,0:T(8,128)(2,1)S(1)}, bf16[1280,128]{1,0:T(8,128)(2,1)S(1)}, u32[]{:S(2)}, u32[]{:S(2)}) collective-permute-start(bf16[1280,128]{1,0:T(8,128)(2,1)S(1)} %get-tuple-element.91), channel_id=1, source_target_pairs={{0,1},{1,0},{2,3},{3,2},{4,5},{5,4},{6,7},{7,6},{8,9},{9,8},{10,11... | collective-permute-start | bytes 983048 | tf_op jit(solution)/shard_map/ppermute | solution.py:57
  89.5 7.2 %copy-start.37 = (bf16[1280,128]{1,0:T(8,128)(2,1)S(1)}, bf16[1280,128]{1,0:T(8,128)(2,1)}, u32[]{:S(2)}) copy-start(bf16[1280,128]{1,0:T(8,128)(2,1)} %param.10) | copy-start | bytes 983044
  91.6 37.4 %collective-permute-start.19 = (bf16[1280,128]{1,0:T(8,128)(2,1)}, bf16[1280,128]{1,0:T(8,128)(2,1)}, u32[]{:S(2)}, u32[]{:S(2)}) collective-permute-start(bf16[1280,128]{1,0:T(8,128)(2,1)} %get-tuple-element.50), channel_id=1, source_target_pairs={{0,1},{1,0},{2,3},{3,2},{4,5},{5,4},{6,7},{7,6},{8,9},{9,8},{10,11... | collective-permute-start | bytes 983048 | tf_op jit(solution)/shard_map/ppermute | solution.py:40
  97.7 45.1 %collective-permute-start.12 = (bf16[1280,128]{1,0:T(8,128)(2,1)}, bf16[1280,128]{1,0:T(8,128)(2,1)}, u32[]{:S(2)}, u32[]{:S(2)}) collective-permute-start(bf16[1280,128]{1,0:T(8,128)(2,1)} %fusion.67), channel_id=1, source_target_pairs={{0,7},{1,6},{2,5},{3,4},{4,11},{5,10},{6,9},{7,8},{8,15},{9,14},{1... | collective-permute-start | bytes 983048 | tf_op jit(solution)/shard_map/ppermute | solution.py:40
  98.8 44.9 %collective-permute-start.11 = (bf16[1280,128]{1,0:T(8,128)(2,1)}, bf16[1280,128]{1,0:T(8,128)(2,1)}, u32[]{:S(2)}, u32[]{:S(2)}) collective-permute-start(bf16[1280,128]{1,0:T(8,128)(2,1)} %fusion.67), channel_id=1, source_target_pairs={{0,6},{1,7},{2,4},{3,5},{4,10},{5,11},{6,8},{7,9},{8,14},{9,15},{1... | collective-permute-start | bytes 983048 | tf_op jit(solution)/shard_map/ppermute | solution.py:40
  126.6 23.0 %collective-permute-start.10 = (bf16[1280,128]{1,0:T(8,128)(2,1)}, bf16[1280,128]{1,0:T(8,128)(2,1)S(1)}, u32[]{:S(2)}, u32[]{:S(2)}) collective-permute-start(bf16[1280,128]{1,0:T(8,128)(2,1)} %fusion.67), channel_id=1, source_target_pairs={{0,5},{1,4},{2,7},{3,6},{4,9},{5,8},{6,11},{7,10},{8,13},{9,12},{1... | collective-permute-start | bytes 983048 | tf_op jit(solution)/shard_map/ppermute | solution.py:40
  127.6 22.0 %collective-permute-start.9 = (bf16[1280,128]{1,0:T(8,128)(2,1)}, bf16[1280,128]{1,0:T(8,128)(2,1)S(1)}, u32[]{:S(2)}, u32[]{:S(2)}) collective-permute-start(bf16[1280,128]{1,0:T(8,128)(2,1)} %fusion.67), channel_id=1, source_target_pairs={{0,4},{1,5},{2,6},{3,7},{4,8},{5,9},{6,10},{7,11},{8,12},{9,13},{1... | collective-permute-start | bytes 983048 | tf_op jit(solution)/shard_map/ppermute | solution.py:40
  129.0 20.6 %collective-permute-start.18 = (bf16[1280,128]{1,0:T(8,128)(2,1)S(1)}, bf16[1280,128]{1,0:T(8,128)(2,1)S(1)}, u32[]{:S(2)}, u32[]{:S(2)}) collective-permute-start(bf16[1280,128]{1,0:T(8,128)(2,1)S(1)} %get-tuple-element.85), channel_id=1, source_target_pairs={{0,3},{1,2},{2,1},{3,0},{4,7},{5,6},{6,5},{7,4},{8,11},{9,10},{10,... | collective-permute-start | bytes 983048 | tf_op jit(solution)/shard_map/ppermute | solution.py:57
  142.7 9.7 %collective-permute-start.17 = (bf16[1280,128]{1,0:T(8,128)(2,1)S(1)}, bf16[1280,128]{1,0:T(8,128)(2,1)S(1)}, u32[]{:S(2)}, u32[]{:S(2)}) collective-permute-start(bf16[1280,128]{1,0:T(8,128)(2,1)S(1)} %get-tuple-element.86), channel_id=1, source_target_pairs={{0,2},{1,3},{2,0},{3,1},{4,6},{5,7},{6,4},{7,5},{8,10},{9,11},{10,... | collective-permute-start | bytes 983048 | tf_op jit(solution)/shard_map/ppermute | solution.py:57
  143.7 4.8 %copy-start.23 = (bf16[5,8,128,128]{3,2,1,0:T(8,128)(2,1)S(1)}, bf16[5,8,128,128]{3,2,1,0:T(8,128)(2,1)}, u32[]{:S(2)}) copy-start(bf16[5,8,128,128]{3,2,1,0:T(8,128)(2,1)} %copy.48) | copy-start | bytes 3932164
  143.7 9.1 %collective-permute-start.16 = (bf16[1280,128]{1,0:T(8,128)(2,1)S(1)}, bf16[1280,128]{1,0:T(8,128)(2,1)S(1)}, u32[]{:S(2)}, u32[]{:S(2)}) collective-permute-start(bf16[1280,128]{1,0:T(8,128)(2,1)S(1)} %get-tuple-element.87), channel_id=1, source_target_pairs={{0,1},{1,0},{2,3},{3,2},{4,5},{5,4},{6,7},{7,6},{8,9},{9,8},{10,11... | collective-permute-start | bytes 983048 | tf_op jit(solution)/shard_map/ppermute | solution.py:57
  149.6 9.2 %copy-start.32 = (bf16[1280,128]{1,0:T(8,128)(2,1)}, bf16[1280,128]{1,0:T(8,128)(2,1)S(1)}, u32[]{:S(2)}) copy-start(bf16[1280,128]{1,0:T(8,128)(2,1)S(1)} %collective-permute-done.9) | copy-start | bytes 983044
  153.1 19.4 %collective-permute-start.28 = (bf16[1280,128]{1,0:T(8,128)(2,1)S(1)}, bf16[1280,128]{1,0:T(8,128)(2,1)S(1)}, u32[]{:S(2)}, u32[]{:S(2)}) collective-permute-start(bf16[1280,128]{1,0:T(8,128)(2,1)S(1)} %fusion.68), channel_id=1, source_target_pairs={{0,31},{1,30},{2,29},{3,28},{4,3},{5,2},{6,1},{7,0},{8,7},{9,6},{1... | collective-permute-start | bytes 983048 | tf_op jit(solution)/shard_map/ppermute | solution.py:40
  154.7 19.2 %collective-permute-start.27 = (bf16[1280,128]{1,0:T(8,128)(2,1)S(1)}, bf16[1280,128]{1,0:T(8,128)(2,1)S(1)}, u32[]{:S(2)}, u32[]{:S(2)}) collective-permute-start(bf16[1280,128]{1,0:T(8,128)(2,1)S(1)} %fusion.68), channel_id=1, source_target_pairs={{0,30},{1,31},{2,28},{3,29},{4,2},{5,3},{6,0},{7,1},{8,6},{9,7},{1... | collective-permute-start | bytes 983048 | tf_op jit(solution)/shard_map/ppermute | solution.py:40
  157.4 17.5 %collective-permute-start.26 = (bf16[1280,128]{1,0:T(8,128)(2,1)S(1)}, bf16[1280,128]{1,0:T(8,128)(2,1)S(1)}, u32[]{:S(2)}, u32[]{:S(2)}) collective-permute-start(bf16[1280,128]{1,0:T(8,128)(2,1)S(1)} %fusion.68), channel_id=1, source_target_pairs={{0,29},{1,28},{2,31},{3,30},{4,1},{5,0},{6,3},{7,2},{8,5},{9,4},{1... | collective-permute-start | bytes 983048 | tf_op jit(solution)/shard_map/ppermute | solution.py:40
  157.8 17.2 %collective-permute-start.25 = (bf16[1280,128]{1,0:T(8,128)(2,1)S(1)}, bf16[1280,128]{1,0:T(8,128)(2,1)S(1)}, u32[]{:S(2)}, u32[]{:S(2)}) collective-permute-start(bf16[1280,128]{1,0:T(8,128)(2,1)S(1)} %fusion.68), channel_id=1, source_target_pairs={{0,28},{1,29},{2,30},{3,31},{4,0},{5,1},{6,2},{7,3},{8,4},{9,5},{1... | collective-permute-start | bytes 983048 | tf_op jit(solution)/shard_map/ppermute | solution.py:40
  170.3 4.8 %copy-start.12 = (bf16[16,320,128]{2,1,0:T(8,128)(2,1)}, bf16[16,320,128]{2,1,0:T(8,128)(2,1)S(1)}, u32[]{:S(2)}) copy-start(bf16[16,320,128]{2,1,0:T(8,128)(2,1)S(1)} %shard_map.144) | copy-start | bytes 3932164
  171.4 66.5 %collective-permute-start.22 = (bf16[1280,128]{1,0:T(8,128)(2,1)}, bf16[1280,128]{1,0:T(8,128)(2,1)}, u32[]{:S(2)}, u32[]{:S(2)}) collective-permute-start(bf16[1280,128]{1,0:T(8,128)(2,1)} %get-tuple-element.82), channel_id=1, source_target_pairs={{0,1},{1,0},{2,3},{3,2},{4,5},{5,4},{6,7},{7,6},{8,9},{9,8},{10,11... | collective-permute-start | bytes 983048 | tf_op jit(solution)/shard_map/ppermute | solution.py:57
  172.5 65.5 %collective-permute-start.24 = (bf16[1280,128]{1,0:T(8,128)(2,1)}, bf16[1280,128]{1,0:T(8,128)(2,1)}, u32[]{:S(2)}, u32[]{:S(2)}) collective-permute-start(bf16[1280,128]{1,0:T(8,128)(2,1)} %get-tuple-element.83), channel_id=1, source_target_pairs={{0,3},{1,2},{2,1},{3,0},{4,7},{5,6},{6,5},{7,4},{8,11},{9,10},{10,... | collective-permute-start | bytes 983048 | tf_op jit(solution)/shard_map/ppermute | solution.py:57
  173.9 64.1 %collective-permute-start.23 = (bf16[1280,128]{1,0:T(8,128)(2,1)}, bf16[1280,128]{1,0:T(8,128)(2,1)}, u32[]{:S(2)}, u32[]{:S(2)}) collective-permute-start(bf16[1280,128]{1,0:T(8,128)(2,1)} %get-tuple-element.84), channel_id=1, source_target_pairs={{0,2},{1,3},{2,0},{3,1},{4,6},{5,7},{6,4},{7,5},{8,10},{9,11},{10,... | collective-permute-start | bytes 983048 | tf_op jit(solution)/shard_map/ppermute | solution.py:57
  188.0 5.9 %copy-start.21 = (bf16[10,8,128,128]{3,2,1,0:T(8,128)(2,1)S(1)}, bf16[10,8,128,128]{3,2,1,0:T(8,128)(2,1)}, u32[]{:S(2)}) copy-start(bf16[10,8,128,128]{3,2,1,0:T(8,128)(2,1)} %copy.47) | copy-start | bytes 7864324
  188.0 5.9 %copy-start.26 = (bf16[1,40,128,128]{2,3,1,0:T(8,128)(2,1)S(1)}, bf16[1,40,128,128]{2,3,1,0:T(8,128)(2,1)}, u32[]{:S(2)}) copy-start(bf16[1,40,128,128]{2,3,1,0:T(8,128)(2,1)} %get-tuple-element.74) | copy-start | bytes 3932164
  188.0 5.9 %copy-start.27 = (bf16[1,40,128,128]{2,3,1,0:T(8,128)(2,1)S(1)}, bf16[1,40,128,128]{2,3,1,0:T(8,128)(2,1)}, u32[]{:S(2)}) copy-start(bf16[1,40,128,128]{2,3,1,0:T(8,128)(2,1)} %get-tuple-element.75) | copy-start | bytes 3932164
  208.5 5.3 %copy-start.7 = (bf16[5120,128]{1,0:T(8,128)(2,1)S(1)}, bf16[5120,128]{1,0:T(8,128)(2,1)}, u32[]{:S(2)}) copy-start(bf16[5120,128]{1,0:T(8,128)(2,1)} %copy-done.6) | copy-start | bytes 3932164
  215.6 5.9 %copy-start.17 = (f32[16,40,320]{2,1,0:T(8,128)S(1)}, f32[16,40,320]{2,1,0:T(8,128)}, u32[]{:S(2)}) copy-start(f32[16,40,320]{2,1,0:T(8,128)} %copy-done.16) | copy-start | bytes 2457604
  224.7 36.9 %all-to-all-start.1 = ((bf16[4,4,3,40,320]{4,3,2,1,0:T(8,128)(2,1)}), bf16[4,4,3,40,320]{4,3,2,1,0:T(8,128)(2,1)S(1)}, u32[]{:S(2)}, u32[]{:S(2)}) async-start(bf16[4,4,3,40,320]{4,3,2,1,0:T(8,128)(2,1)} %bitcast.325), calls=%async_computation.1 | async-start | bytes 2949120 | tf_op jit(solution)/shard_map/all_to_all | solution.py:346
  234.4 26.3 %copy-start.35 = (bf16[1280,128]{1,0:T(8,128)(2,1)S(1)}, bf16[1280,128]{1,0:T(8,128)(2,1)}, u32[]{:S(2)}) copy-start(bf16[1280,128]{1,0:T(8,128)(2,1)} %copy-done.34) | copy-start | bytes 983044
  234.4 20.5 %collective-permute-start.29 = (bf16[1280,128]{1,0:T(8,128)(2,1)S(1)}, bf16[1280,128]{1,0:T(8,128)(2,1)S(1)}, u32[]{:S(2)}, u32[]{:S(2)}) collective-permute-start(bf16[1280,128]{1,0:T(8,128)(2,1)S(1)} %get-tuple-element.79), channel_id=1, source_target_pairs={{0,1},{1,0},{2,3},{3,2},{4,5},{5,4},{6,7},{7,6},{8,9},{9,8},{10,11... | collective-permute-start | bytes 983048 | tf_op jit(solution)/shard_map/ppermute | solution.py:57
  236.5 24.2 %collective-permute-start.31 = (bf16[1280,128]{1,0:T(8,128)(2,1)S(1)}, bf16[1280,128]{1,0:T(8,128)(2,1)S(1)}, u32[]{:S(2)}, u32[]{:S(2)}) collective-permute-start(bf16[1280,128]{1,0:T(8,128)(2,1)S(1)} %get-tuple-element.80), channel_id=1, source_target_pairs={{0,3},{1,2},{2,1},{3,0},{4,7},{5,6},{6,5},{7,4},{8,11},{9,10},{10,... | collective-permute-start | bytes 983048 | tf_op jit(solution)/shard_map/ppermute | solution.py:57
  237.9 22.8 %collective-permute-start.30 = (bf16[1280,128]{1,0:T(8,128)(2,1)S(1)}, bf16[1280,128]{1,0:T(8,128)(2,1)S(1)}, u32[]{:S(2)}, u32[]{:S(2)}) collective-permute-start(bf16[1280,128]{1,0:T(8,128)(2,1)S(1)} %get-tuple-element.81), channel_id=1, source_target_pairs={{0,2},{1,3},{2,0},{3,1},{4,6},{5,7},{6,4},{7,5},{8,10},{9,11},{10,... | collective-permute-start | bytes 983048 | tf_op jit(solution)/shard_map/ppermute | solution.py:57
  (25 other events, 52.4 us)

commit v2 on v1

--- a/solution.py
+++ b/solution.py
@@ -1,3 +1,4 @@
+import functools
 import math
 
 import jax
@@ -63,31 +64,32 @@
     return sum(piece.astype(F32) for piece in pieces)
 
 
-def wide_of(factor):
-    a, width = factor.shape
+def wide_of(factor, first, a):
+    width = factor.shape[1]
+    factor = factor.astype(F32)[first : first + a]
     block = lax.broadcasted_iota(jnp.int32, (JOIN, width), 0) * FIRST_IN
     column = lax.broadcasted_iota(jnp.int32, (JOIN, width), 1)
     keep = (column >= block) & (column < block + FIRST_IN)
-    spread = jnp.broadcast_to(factor.astype(F32)[:, None, :], (a, JOIN, width))
+    spread = jnp.broadcast_to(factor[:, None, :], (a, JOIN, width))
     return jnp.where(keep[None], spread, 0.0).reshape(a * JOIN, width)
 
 
-def by_r_kernel(factor_ref, values_ref, out_ref):
-    a = factor_ref.shape[1]
+def by_r_kernel(first, factor_ref, values_ref, out_ref):
+    a = out_ref.shape[0]
     t = values_ref.shape[2]
     parts = []
     for i in range(PAIR):
-        wide = wide_of(factor_ref[i]).astype(BF16)
+        wide = wide_of(factor_ref[i], first, a).astype(BF16)
         out = jnp.dot(wide, values_ref[i], preferred_element_type=F32)
         parts.append(out.reshape(a, JOIN, t))
     out_ref[...] = jnp.concatenate(parts, axis=1).astype(BF16)
 
 
-def by_p_kernel(factor_ref, rows_ref, out_ref):
+def by_p_kernel(first, factor_ref, rows_ref, out_ref):
     rows = rows_ref[...].astype(F32)
     a, _, t = rows.shape
     for i in range(PAIR):
-        wide = wide_of(factor_ref[i]).astype(BF16)
+        wide = wide_of(factor_ref[i], first, a).astype(BF16)
         mine = rows[:, i * JOIN : (i + 1) * JOIN].reshape(a * JOIN, t).astype(BF16)
         out = lax.dot_general(wide, mine, (((0,), (0,)), ((), ())), preferred_element_type=F32)
         out_ref[i] = out.astype(BF16)
@@ -170,6 +172,55 @@
         cost_estimate=pl.CostEstimate(flops=flops, bytes_accessed=moved, transcendentals=0),
         compiler_params=pltpu.CompilerParams(vmem_limit_bytes=40 * 1024 * 1024),
     )(*operands)
+
+
+def backward_kernel(mixed_ref, grad_ref, up_ref, down_ref, out_mixed_ref, out_ref):
+    for r in range(grad_ref.shape[0]):
+        gate, up = mixed_ref[0, r], mixed_ref[1, r]
+        grad_hidden = jnp.dot(down_ref[r], grad_ref[r], preferred_element_type=F32)
+        sg = 1.0 / (1.0 + jnp.exp(-gate))
+        pair = (grad_hidden * up * (sg * (1.0 + gate * (1.0 - sg))), grad_hidden * gate * sg)
+        for g in range(2):
+            turned = pair[g].astype(BF16)
+            out_mixed_ref[g, r] = turned
+            out = jnp.dot(up_ref[g, r], turned, preferred_element_type=F32)
+            out_ref[g, r] = out.astype(BF16)
+
+
+def weight_kernel(factor, *refs):
+    half = (len(refs) - 2) // 2
+    out_ref, held_ref = refs[-2:]
+    count, high, _ = refs[0].shape
+    for a in range(count):
+        left = jnp.concatenate([ref[a] for ref in refs[:half]], axis=1)
+        right = jnp.concatenate([ref[a] for ref in refs[half : 2 * half]], axis=1)
+        held_ref[a * high : (a + 1) * high] = factor * lax.dot_general(
+            left, right, (((1,), (1,)), ((), ())), preferred_element_type=F32
+        )
+    wide = held_ref.shape[1]
+    for m in range(high):
+        row = held_ref[pl.ds(m, count, stride=high), :]
+        out_ref[:, m * wide : (m + 1) * wide] = row.astype(BF16)
+
+
+def weight_call(lefts, rights, factor):
+    total, high, t = lefts[0].shape
+    wide = rights[0].shape[1]
+    count = 16 if total % 16 == 0 else total
+    return pl.pallas_call(
+        functools.partial(weight_kernel, factor),
+        grid=(total // count,),
+        in_specs=[pl.BlockSpec((count,) + x.shape[1:], lead) for x in (*lefts, *rights)],
+        out_specs=pl.BlockSpec((count, high * wide), lambda i: (i, 0)),
+        out_shape=jax.ShapeDtypeStruct((total, high * wide), BF16),
+        scratch_shapes=[pltpu.VMEM((count * high, wide), F32)],
+        cost_estimate=pl.CostEstimate(
+            flops=2 * len(lefts) * total * high * wide * t,
+            bytes_accessed=2 * total * (high * wide + 2 * len(lefts) * high * t),
+            transcendentals=0,
+        ),
+        compiler_params=pltpu.CompilerParams(vmem_limit_bytes=48 * 1024 * 1024),
+    )(*lefts, *rights)
 
 
 def lead(i):
@@ -219,33 +270,33 @@
     )
     factors = lax.all_to_all(cut, "blk", split_axis=0, concat_axis=0, tiled=True)
     factors = factors.reshape(groups, 3 * own_r, width)
-    up_factor, down_factor = factors[:, : 2 * own_r], factors[:, 2 * own_r :]
+    up_factor, down_factor = (0, 2 * own_r), (2 * own_r, own_r)
     up_second = second_up[0].reshape(2, own_r, FIRST_BLOCKS, -1)
     down_first = first_down[0].reshape(own_r, -1, FIRST_BLOCKS)
 
     def by_r(factor, values):
-        a, t = factor.shape[1], values.shape[1]
+        (first, a), t = factor, values.shape[1]
         return call(
-            by_r_kernel,
+            functools.partial(by_r_kernel, first),
             2 * a * FIRST_BLOCKS * width * t,
             (a, FIRST_BLOCKS, t),
             (a, PAIR * JOIN, t),
             middle_dim,
-            (factor, values.reshape(groups, width, t)),
-            ((PAIR, a, width), (PAIR, width, t)),
+            (factors, values.reshape(groups, width, t)),
+            ((PAIR, 3 * own_r, width), (PAIR, width, t)),
             (lead, lead),
         )
 
     def by_p(factor, values):
         a, _, t = values.shape
         return call(
-            by_p_kernel,
+            functools.partial(by_p_kernel, factor[0]),
             2 * a * FIRST_BLOCKS * width * t,
             (groups, width, t),
             (PAIR, width, t),
             lead,
-            (factor, values),
-            ((PAIR, a, width), (a, PAIR * JOIN, t)),
+            (factors, values),
+            ((PAIR, 3 * own_r, width), (a, PAIR * JOIN, t)),
             (lead, middle_dim),
         ).reshape(n, rows, t)
 
@@ -272,17 +323,28 @@
         return spread, mixed, hidden, lowered.astype(BF16)
 
     def backward(grad_lowered, mixed):
-        grad_hidden = jnp.einsum(
-            "rop,rpt->rot", down_first, grad_lowered, preferred_element_type=F32
-        )
-        sg = jax.nn.sigmoid(mixed[0])
-        slope = sg * (1.0 + mixed[0] * (1.0 - sg))
-        grad_mixed = jnp.stack(
-            [grad_hidden * mixed[1] * slope, grad_hidden * mixed[0] * sg]
-        ).astype(BF16)
-        grad_spread = jnp.einsum(
-            "grpo,grot->grpt", up_second, grad_mixed, preferred_element_type=F32
-        ).astype(BF16)
+        count = 8 if own_r % 8 == 0 else own_r
+        four = lambda i: (0, i, 0, 0)
+        wide = mixed.shape[2]
+        shapes = ((2, own_r, wide, tokens), (2, own_r, FIRST_BLOCKS, tokens))
+        grad_mixed, grad_spread = pl.pallas_call(
+            backward_kernel,
+            grid=(own_r // count,),
+            in_specs=[
+                pl.BlockSpec((2, count, wide, tokens), four),
+                pl.BlockSpec((count, FIRST_BLOCKS, tokens), lead),
+                pl.BlockSpec((2, count, FIRST_BLOCKS, wide), four),
+                pl.BlockSpec((count, wide, FIRST_BLOCKS), lead),
+            ],
+            out_specs=[pl.BlockSpec((2, count) + x[2:], four) for x in shapes],
+            out_shape=[jax.ShapeDtypeStruct(x, BF16) for x in shapes],
+            cost_estimate=pl.CostEstimate(
+                flops=6 * own_r * FIRST_BLOCKS * wide * tokens,
+                bytes_accessed=20 * own_r * wide * tokens,
+                transcendentals=own_r * wide * tokens,
+            ),
+            compiler_params=pltpu.CompilerParams(vmem_limit_bytes=40 * 1024 * 1024),
+        )(mixed, grad_lowered, up_second, down_first)
         return grad_mixed, grad_spread.reshape(-1, FIRST_BLOCKS, tokens)
 
     def add(values, added):
@@ -290,23 +352,18 @@
 
     factor = 1.0 / math.sqrt(TICKS * tokens)
 
-    def terms_of(stash, stash_all, grads_all, grad_lowered, grad_mixed, grad_spread):
-        spread, _, hidden, lowered = stash
-        return (
-            term_of(grad_spread, stash_all),
-            term_of(lowered, grads_all),
-            jnp.einsum("grpt,grot->grpo", spread, grad_mixed, preferred_element_type=F32),
-            jnp.einsum("rot,rpt->rop", hidden, grad_lowered, preferred_element_type=F32),
-        )
+    def terms_of(stash, stash_all, grads_all, grad_spread):
+        return term_of(grad_spread, stash_all), term_of(stash[3], grads_all)
 
     inputs, grads = held_input[0], held_grad[0]
     input_pieces = spread_over(inputs, n, 0)
-    grad_pieces = spread_over(grads, n, 0)
+    grad_pieces = spread_over(lax.optimization_barrier((grads, factors[0]))[0], n, 0)
     stash_pieces = [
         spread_over(lax.optimization_barrier((stashed[0, k], factors[0]))[0], n, 0)
         for k in range(TICKS)
     ]
     totals = stash = None
+    seen = []
     outputs = back = forward_pieces = backward_pieces = None
     for k in range(TICKS):
         lowered = middle(placed(input_pieces, n, me))[3]
@@ -324,7 +381,9 @@
         grads_all = placed(grad_pieces, n, me)
         grad_lowered = by_r(down_factor, grads_all)
         grad_mixed, grad_spread = backward(grad_lowered, stash[1])
-        backward_pieces = send(by_p(up_factor, grad_spread), n, me)
+        pieces = by_p(up_factor, grad_spread)
+        backward_pieces = send(pieces, n, me)
+        seen.append((stash[0].reshape(-1, FIRST_BLOCKS, tokens), stash[2], grad_lowered, grad_mixed))
         if k + 1 < TICKS:
             next_pieces, _ = lax.optimization_barrier((stash_pieces[k + 1], backward_pieces[0]))
             next_all = placed(next_pieces, n, me)
@@ -335,15 +394,22 @@
             inputs = input_pieces[0]
             back = add(grads, total_of(backward_pieces))
             grad_pieces = spread_over(jnp.where(section_pos == 0, fresh_grad, back), n, -1)
-            terms = terms_of(stash, stash_all, grads_all, grad_lowered, grad_mixed, grad_spread)
+            terms = terms_of(stash, stash_all, grads_all, grad_spread)
             totals = terms if totals is None else [x + y for x, y in zip(totals, terms)]
             grad_pieces, totals = lax.optimization_barrier((grad_pieces, totals))
             grads = grad_pieces[0]
             stash, stash_all = next_stash, next_all
-    terms = terms_of(stash, stash_all, grads_all, grad_lowered, grad_mixed, grad_spread)
-    t1, t4, w2, w3 = (((x + y) * factor).astype(BF16) for x, y in zip(totals, terms))
+    grad_spread, _ = lax.optimization_barrier((grad_spread, pieces))
+    terms = terms_of(stash, stash_all, grads_all, grad_spread)
+    t1, t4 = (((x + y) * factor).astype(BF16) for x, y in zip(totals, terms))
     back_cut = jnp.concatenate([t1, t4], axis=1).reshape(cut_dims)
+    seen, back_cut = lax.optimization_barrier((seen, back_cut))
+    spreads, hiddens, grads_lowered, grads_mixed = zip(*seen)
+    grads_mixed = [x.reshape(2 * own_r, -1, tokens) for x in grads_mixed]
     small = lax.all_to_all(back_cut, "blk", split_axis=0, concat_axis=0, tiled=True)
+    w2 = weight_call(spreads, grads_mixed, factor)
+    w3 = weight_call(hiddens, grads_lowered, factor)
+    small, backward_pieces, w2, w3 = lax.optimization_barrier((small, backward_pieces, w2, w3))
     back = add(grads, total_of(backward_pieces))
     small = lax.optimization_barrier(small)
     g1 = relay_call(

time: 274 us -> 267 us (0.974)
  Pallas kernels: 57.7 us -> 86.8 us
  waiting for transfers between devices: 43.8 us -> 71.6 us
  matrix products: 33.1 us -> 7.81 us
  local copies, waits for them, and re-layouts: 61.2 us -> 37.3 us
  other arithmetic: 14.1 us -> 7.5 us
  starting transfers between devices: 56.8 us -> 50.2 us
    pallas_call x0 -> x4, Pallas kernels: none -> 29.6 us  [the longest x2 18.1 us: backward(): pl.pallas_call(backward_kernel, grid=(own_r // count,), in_specs=[pl.Bloc...]
    dot_general x8 -> x0, matrix products: 23.4 us -> none  [the longest x2 9.12 us: terms_of(): jnp.einsum('grpt,grot->grpo', spread, grad_mixed, preferred_element_type=...]
    ppermute x12, waiting for transfers between devices: 28.7 us -> 50.8 us  [send(): lax.ppermute(mine, 'blk', [(i, partner_of(i, d, n)) for i in range(n)])]
    convert_element_type x2 -> x0, local copies, waits for them, and re-layouts: 8.81 us -> none  [backward(): grad_spread = jnp.einsum('grpo,grot->grpt', up_second, grad_mixed, prefer...]
    convert_element_type x4 -> x2, other arithmetic: 7.71 us -> 0.47 us  [shards(): t1, t4 = (((x + y) * factor).astype(BF16) for x, y in zip(totals, terms))]
    ppermute x12, starting transfers between devices: 20.2 us -> 13.2 us  [send(): lax.ppermute(mine, 'blk', [(i, partner_of(i, d, n)) for i in range(n)])]
    reshape x2 -> x0, local copies, waits for them, and re-layouts: 6.89 us -> none  [the longest x1 5.28 us: shards(): w2.reshape(second_up.shape)]
    dynamic_update_slice x23, local copies, waits for them, and re-layouts: 11.8 us -> 6.21 us  [placed(): lax.dynamic_update_slice_in_dim(whole, piece, source_of(me, d, n) * rows, 0)]
  transfers between devices with their start and end apart: 34 -> 34, of which waited for: 7 -> 16; matrix products, arithmetic and copies ran while one was open for 34% -> 12% of each run, Pallas kernels for 21% -> 23%
where the time goes in v2:
time: 267 us; the launch traced here: 263 us
  Pallas kernels  86.8 us (33%)
  waiting for transfers between devices  71.6 us (27%)
  starting transfers between devices  50.2 us (19%)
  local copies, waits for them, and re-layouts  37.3 us (14%)
  matrix products  7.81 us (3%)
  other arithmetic  7.5 us (3%)
    pallas_call x14, Pallas kernels, call(): pl.pallas_call(kernel, grid=(FIRST_BLOCKS // (PAIR * JOIN),), in_specs=[p...  52.8 us
    ppermute x12, waiting for transfers between devices, send(): lax.ppermute(mine, 'blk', [(i, partner_of(i, d, n)) for i in range(n)])  50.8 us
    ppermute x20, starting transfers between devices, spread_over(): arrived.append(lax.ppermute(value, ('section', 'blk'), pairs))  27.9 us
    pallas_call x2, Pallas kernels, backward(): pl.pallas_call(backward_kernel, grid=(own_r // count,), in_specs=[pl.Bloc...  18.1 us
    ppermute x20, waiting for transfers between devices, spread_over(): arrived.append(lax.ppermute(value, ('section', 'blk'), pairs))  17.7 us
    unnamed x78, local copies, waits for them, and re-layouts  16.7 us
    ppermute x12, starting transfers between devices, send(): lax.ppermute(mine, 'blk', [(i, partner_of(i, d, n)) for i in range(n)])  13.2 us
    pallas_call x2, Pallas kernels, weight_call(): pl.pallas_call(functools.partial(weight_kernel, factor), grid=(total // c...  11.5 us
  transfers between devices with their start and end apart: 34, of which 16 were waited for; matrix products, arithmetic and copies ran while one was open for 12% of the time, Pallas kernels for 23%

profile of v2, /device:TPU:0, one launch (start us, length us, event | category | flops | bytes accessed | tf_op | source)
XLA Modules:
  0.0 263.0 jit_solution(14305468716931399940)
XLA Ops:
  0.6 3.0 %collective-permute-start = (bf16[1280,128]{1,0:T(8,128)(2,1)}, bf16[1280,128]{1,0:T(8,128)(2,1)}, u32[]{:S(2)}, u32[]{:S(2)}) collective-permute-start(bf16[1280,128]{1,0:T(8,128)(2,1)} %bitcast.231), channel_id=1, source_target_pairs={{0,1},{1,0},{2,3},{3,2},{4,5},{5,4},{6,7},{7,6},{8,9},{9,8},{10,11... | collective-permute-start | bytes 983048 | tf_op jit(solution)/shard_map/ppermute | solution.py:41
  5.2 3.4 %reshape_squeeze.12 = bf16[4,8,4,40,40]{4,3,2,1,0:T(8,128)(2,1)S(1)} reshape(bf16[1,32,6400]{2,1,0:T(8,128)(2,1)} %param.17) | data formatting | bytes 819200 | tf_op jit(solution)/shard_map/reshape;squeeze | solution.py:260
  10.2 2.2 shard_map.136
  12.5 4.5 %all-to-all-start = ((bf16[4,4,3,40,320]{4,3,2,1,0:T(8,128)(2,1)}), bf16[4,4,3,40,320]{4,3,2,1,0:T(8,128)(2,1)S(1)}, u32[]{:S(2)}, u32[]{:S(2)}) async-start(bf16[4,4,3,40,320]{4,3,2,1,0:T(8,128)(2,1)} %shard_map.136), calls=%async_computation | async-start | bytes 2949120 | tf_op jit(solution)/shard_map/all_to_all | solution.py:271
  19.1 1.8 copy.50
  21.3 2.2 copy.49
  23.5 1.8 constant_dynamic-update-slice_fusion.22
  25.3 5.3 %collective-permute-done.1 = bf16[1280,128]{1,0:T(8,128)(2,1)} collective-permute-done((bf16[1280,128]{1,0:T(8,128)(2,1)}, bf16[1280,128]{1,0:T(8,128)(2,1)}, u32[]{:S(2)}, u32[]{:S(2)}) %collective-permute-start.1) | collective-permute-done | bytes 327712 | tf_op jit(solution)/shard_map/ppermute | solution.py:41
  34.0 3.1 %all-to-all-done = bf16[4,4,3,40,320]{4,3,2,1,0:T(8,128)(2,1)S(1)} async-done(((bf16[4,4,3,40,320]{4,3,2,1,0:T(8,128)(2,1)}), bf16[4,4,3,40,320]{4,3,2,1,0:T(8,128)(2,1)S(1)}, u32[]{:S(2)}, u32[]{:S(2)}) %all-to-all-start) | async-done | bytes 1228832 | tf_op jit(solution)/shard_map/all_to_all | solution.py:271
  44.8 3.6 %shard_map.137 = bf16[80,128,128]{2,1,0:T(8,128)(2,1)S(1)} custom-call(bf16[16,120,320]{2,1,0:T(8,128)(2,1)S(1)} %bitcast.177, bf16[16,320,128]{2,1,0:T(8,128)(2,1)S(1)} %bitcast.218), custom_call_target="tpu_custom_call" | custom-call | flops 838860800 | bytes 5160960 | tf_op jit(solution)/shard_map/pallas_call | solution.py:166
  51.0 3.1 %shard_map.138 = bf16[16,320,128]{2,1,0:T(8,128)(2,1)S(1)} custom-call(bf16[16,120,320]{2,1,0:T(8,128)(2,1)S(1)} %bitcast.178, bf16[40,128,128]{2,1,0:T(8,128)(2,1)S(1)} %fusion.8.rows_ref), custom_call_target="tpu_custom_call" | custom-call | flops 419430400 | bytes 3850240 | tf_op jit(solution)/shard_map/pallas_call | solution.py:166
  57.3 4.3 %collective-permute-start.20 = (bf16[1280,128]{1,0:T(8,128)(2,1)S(1)}, bf16[1280,128]{1,0:T(8,128)(2,1)S(1)}, u32[]{:S(2)}, u32[]{:S(2)}) collective-permute-start(bf16[1280,128]{1,0:T(8,128)(2,1)S(1)} %copy-done.27), channel_id=1, source_target_pairs={{0,2},{1,3},{2,0},{3,1},{4,6},{5,7},{6,4},{7,5},{8,10},{9,11},{10,... | collective-permute-start | bytes 983048 | tf_op jit(solution)/shard_map/ppermute | solution.py:41
  62.0 6.9 %collective-permute-done.13 = bf16[1280,128]{1,0:T(8,128)(2,1)S(1)} collective-permute-done((bf16[1280,128]{1,0:T(8,128)(2,1)S(1)}, bf16[1280,128]{1,0:T(8,128)(2,1)S(1)}, u32[]{:S(2)}, u32[]{:S(2)}) %collective-permute-start.13) | collective-permute-done | bytes 327712 | tf_op jit(solution)/shard_map/ppermute | solution.py:41
  68.9 2.6 collective-permute-start.5
  72.7 3.6 %shard_map.139.refs_0_ = bf16[80,128,128]{2,1,0:T(8,128)(2,1)S(1)} custom-call(bf16[16,120,320]{2,1,0:T(8,128)(2,1)S(1)} %bitcast.179, bf16[16,320,128]{2,1,0:T(8,128)(2,1)S(1)} %bitcast.205), custom_call_target="tpu_custom_call" | custom-call | flops 838860800 | bytes 5160960 | tf_op jit(solution)/shard_map/pallas_call | solution.py:166
  81.2 2.8 %collective-permute-done.5 = bf16[1280,128]{1,0:T(8,128)(2,1)S(1)} collective-permute-done((bf16[1280,128]{1,0:T(8,128)(2,1)S(1)}, bf16[1280,128]{1,0:T(8,128)(2,1)S(1)}, u32[]{:S(2)}, u32[]{:S(2)}) %collective-permute-start.5) | collective-permute-done | bytes 327712 | tf_op jit(solution)/shard_map/ppermute | solution.py:58
  85.5 10.2 %collective-permute-done.4 = bf16[1280,128]{1,0:T(8,128)(2,1)S(1)} collective-permute-done((bf16[1280,128]{1,0:T(8,128)(2,1)S(1)}, bf16[1280,128]{1,0:T(8,128)(2,1)S(1)}, u32[]{:S(2)}, u32[]{:S(2)}) %collective-permute-start.4) | collective-permute-done | bytes 327712 | tf_op jit(solution)/shard_map/ppermute | solution.py:58
  97.1 1.9 collective-permute-start.11
  99.0 2.4 shard_map.140.grad_ref.refs_2_
  101.5 9.3 %shard_map.141 = (bf16[2,40,128,128]{3,2,1,0:T(8,128)(2,1)S(1)}, bf16[2,40,128,128]{3,2,1,0:T(8,128)(2,1)S(1)}) custom-call(f32[2,40,128,128]{3,2,1,0:T(8,128)} %copy-done.23, bf16[40,128,128]{2,1,0:T(8,128)(2,1)S(1)} %shard_map.140.grad_ref.refs_2_, bf16[2,40,128,128]{3,2,1,0:T(8,128)(2,1)S(1)} %bitcast.189, bf16[40,128,128]{2,1,0:T(8,128)(2,1)S(1)} %bitcast.195), custom_call_target="tpu_custom_call" | custom-call | flops 503316480 | bytes 13107200 | tf_op jit(solution)/shard_map/pallas_call | solution.py:330
  112.3 5.8 %shard_map.146 = f32[16,80,320]{2,1,0:T(8,128)S(1)} custom-call(bf16[80,128,128]{2,1,0:T(8,128)(2,1)S(1)} %bitcast.213, bf16[16,320,128]{2,1,0:T(8,128)(2,1)S(1)} %bitcast.206), custom_call_target="tpu_custom_call" | custom-call | flops 838860800 | bytes 4751360 | tf_op jit(solution)/shard_map/pallas_call | solution.py:166
  118.1 4.3 %shard_map.142 = bf16[16,320,128]{2,1,0:T(8,128)(2,1)S(1)} custom-call(bf16[16,120,320]{2,1,0:T(8,128)(2,1)S(1)} %bitcast.181, bf16[80,128,128]{2,1,0:T(8,128)(2,1)S(1)} %bitcast.214), custom_call_target="tpu_custom_call" | custom-call | flops 838860800 | bytes 5160960 | tf_op jit(solution)/shard_map/pallas_call | solution.py:166
  126.0 3.6 %shard_map.143 = bf16[80,128,128]{2,1,0:T(8,128)(2,1)S(1)} custom-call(bf16[16,120,320]{2,1,0:T(8,128)(2,1)S(1)} %bitcast.182, bf16[16,320,128]{2,1,0:T(8,128)(2,1)S(1)} %bitcast.207), custom_call_target="tpu_custom_call" | custom-call | flops 838860800 | bytes 5160960 | tf_op jit(solution)/shard_map/pallas_call | solution.py:166
  133.5 7.3 %collective-permute-done.18 = bf16[1280,128]{1,0:T(8,128)(2,1)S(1)} collective-permute-done((bf16[1280,128]{1,0:T(8,128)(2,1)S(1)}, bf16[1280,128]{1,0:T(8,128)(2,1)S(1)}, u32[]{:S(2)}, u32[]{:S(2)}) %collective-permute-start.18) | collective-permute-done | bytes 327712 | tf_op jit(solution)/shard_map/ppermute | solution.py:58
  143.0 3.5 %shard_map.147 = f32[16,40,320]{2,1,0:T(8,128)S(1)} custom-call(bf16[40,128,128]{2,1,0:T(8,128)(2,1)S(1)} %fusion.9.rows_ref, bf16[16,320,128]{2,1,0:T(8,128)(2,1)S(1)} %bitcast.204), custom_call_target="tpu_custom_call" | custom-call | flops 419430400 | bytes 3031040 | tf_op jit(solution)/shard_map/pallas_call | solution.py:166
  147.2 5.1 %collective-permute-done.16 = bf16[1280,128]{1,0:T(8,128)(2,1)S(1)} collective-permute-done((bf16[1280,128]{1,0:T(8,128)(2,1)S(1)}, bf16[1280,128]{1,0:T(8,128)(2,1)S(1)}, u32[]{:S(2)}, u32[]{:S(2)}) %collective-permute-start.16) | collective-permute-done | bytes 327712 | tf_op jit(solution)/shard_map/ppermute | solution.py:58
  152.6 2.0 collective-permute-start.28
  158.0 3.6 %shard_map.144 = bf16[80,128,128]{2,1,0:T(8,128)(2,1)S(1)} custom-call(bf16[16,120,320]{2,1,0:T(8,128)(2,1)S(1)} %bitcast.183, bf16[16,320,128]{2,1,0:T(8,128)(2,1)S(1)} %bitcast.219), custom_call_target="tpu_custom_call" | custom-call | flops 838860800 | bytes 5160960 | tf_op jit(solution)/shard_map/pallas_call | solution.py:166
  163.9 3.1 %shard_map.145 = bf16[16,320,128]{2,1,0:T(8,128)(2,1)S(1)} custom-call(bf16[16,120,320]{2,1,0:T(8,128)(2,1)S(1)} %bitcast.184, bf16[40,128,128]{2,1,0:T(8,128)(2,1)S(1)} %fusion.11.rows_ref), custom_call_target="tpu_custom_call" | custom-call | flops 419430400 | bytes 3850240 | tf_op jit(solution)/shard_map/pallas_call | solution.py:166
  167.2 3.4 %collective-permute-done.27 = bf16[1280,128]{1,0:T(8,128)(2,1)S(1)} collective-permute-done((bf16[1280,128]{1,0:T(8,128)(2,1)S(1)}, bf16[1280,128]{1,0:T(8,128)(2,1)S(1)}, u32[]{:S(2)}, u32[]{:S(2)}) %collective-permute-start.27) | collective-permute-done | bytes 327712 | tf_op jit(solution)/shard_map/ppermute | solution.py:41
  172.3 2.4 shard_map.148.grad_ref.refs_3_
  174.8 3.5 %shard_map.152 = f32[16,40,320]{2,1,0:T(8,128)S(1)} custom-call(bf16[40,128,128]{2,1,0:T(8,128)(2,1)S(1)} %fusion.10.rows_ref, bf16[16,320,128]{2,1,0:T(8,128)(2,1)S(1)} %bitcast.202), custom_call_target="tpu_custom_call" | custom-call | flops 419430400 | bytes 3031040 | tf_op jit(solution)/shard_map/pallas_call | solution.py:166
  178.3 8.8 %shard_map.149 = (bf16[2,40,128,128]{3,2,1,0:T(8,128)(2,1)S(1)}, bf16[2,40,128,128]{3,2,1,0:T(8,128)(2,1)S(1)}) custom-call(f32[2,40,128,128]{3,2,1,0:T(8,128)} %copy-done.22, bf16[40,128,128]{2,1,0:T(8,128)(2,1)S(1)} %shard_map.148.grad_ref.refs_3_, bf16[2,40,128,128]{3,2,1,0:T(8,128)(2,1)S(1)} %bitcast.192, bf16[40,128,128]{2,1,0:T(8,128)(2,1)S(1)} %bitcast.198), custom_call_target="tpu_custom_call" | custom-call | flops 503316480 | bytes 13107200 | tf_op jit(solution)/shard_map/pallas_call | solution.py:330
  187.2 4.3 %shard_map.150 = bf16[16,320,128]{2,1,0:T(8,128)(2,1)S(1)} custom-call(bf16[16,120,320]{2,1,0:T(8,128)(2,1)S(1)} %bitcast.186, bf16[80,128,128]{2,1,0:T(8,128)(2,1)S(1)} %bitcast.211), custom_call_target="tpu_custom_call" | custom-call | flops 838860800 | bytes 5160960 | tf_op jit(solution)/shard_map/pallas_call | solution.py:166
  192.5 5.8 %shard_map.151 = f32[16,80,320]{2,1,0:T(8,128)S(1)} custom-call(bf16[80,128,128]{2,1,0:T(8,128)(2,1)S(1)} %bitcast.212, bf16[16,320,128]{2,1,0:T(8,128)(2,1)S(1)} %bitcast.208), custom_call_target="tpu_custom_call" | custom-call | flops 838860800 | bytes 4751360 | tf_op jit(solution)/shard_map/pallas_call | solution.py:166
  201.5 4.5 %all-to-all-start.1 = ((bf16[4,4,3,40,320]{4,3,2,1,0:T(8,128)(2,1)}), bf16[4,4,3,40,320]{4,3,2,1,0:T(8,128)(2,1)S(1)}, u32[]{:S(2)}, u32[]{:S(2)}) async-start(bf16[4,4,3,40,320]{4,3,2,1,0:T(8,128)(2,1)} %bitcast.225), calls=%async_computation.1 | async-start | bytes 2949120 | tf_op jit(solution)/shard_map/all_to_all | solution.py:409
  207.4 2.3 collective-permute-start.22
  212.8 2.5 collective-permute-start.31
  216.2 3.5 %shard_map.154 = bf16[40,16384]{1,0:T(8,128)(2,1)} custom-call(bf16[40,128,128]{2,1,0:T(8,128)(2,1)S(1)} %copy-done.10, bf16[40,128,128]{2,1,0:T(8,128)(2,1)S(1)} %copy-done.12, bf16[40,128,128]{2,1,0:T(8,128)(2,1)S(1)} %copy-done.6, bf16[40,128,128]{2,1,0:T(8,128)(2,1)S(1)} %copy-done.8), custom_call_target="tpu_custom_call" | custom-call | flops 335544320 | bytes 6553600 | tf_op jit(solution)/shard_map/pallas_call | solution.py:210
  219.7 8.0 %shard_map.153 = bf16[80,16384]{1,0:T(8,128)(2,1)} custom-call(bf16[80,128,128]{2,1,0:T(8,128)(2,1)S(1)} %copy-done.2, bf16[80,128,128]{2,1,0:T(8,128)(2,1)S(1)} %copy-done.4, bf16[80,128,128]{2,1,0:T(8,128)(2,1)} %bitcast.222, bf16[80,128,128]{2,1,0:T(8,128)(2,1)} %bitcast.223), custom_call_target="tpu_custom_call" | custom-call | flops 671088640 | bytes 13107200 | tf_op jit(solution)/shard_map/pallas_call | solution.py:210
  227.7 5.2 %collective-permute-done.22 = bf16[1280,128]{1,0:T(8,128)(2,1)S(1)} collective-permute-done((bf16[1280,128]{1,0:T(8,128)(2,1)S(1)}, bf16[1280,128]{1,0:T(8,128)(2,1)S(1)}, u32[]{:S(2)}, u32[]{:S(2)}) %collective-permute-start.22) | collective-permute-done | bytes 327712 | tf_op jit(solution)/shard_map/ppermute | solution.py:58
  232.9 7.7 %collective-permute-done.24 = bf16[1280,128]{1,0:T(8,128)(2,1)S(1)} collective-permute-done((bf16[1280,128]{1,0:T(8,128)(2,1)S(1)}, bf16[1280,128]{1,0:T(8,128)(2,1)S(1)}, u32[]{:S(2)}, u32[]{:S(2)}) %collective-permute-start.24) | collective-permute-done | bytes 327712 | tf_op jit(solution)/shard_map/ppermute | solution.py:58
  240.6 1.9 fusion.21
  242.5 5.1 %collective-permute-done.31 = bf16[1280,128]{1,0:T(8,128)(2,1)S(1)} collective-permute-done((bf16[1280,128]{1,0:T(8,128)(2,1)S(1)}, bf16[1280,128]{1,0:T(8,128)(2,1)S(1)}, u32[]{:S(2)}, u32[]{:S(2)}) %collective-permute-start.31) | collective-permute-done | bytes 327712 | tf_op jit(solution)/shard_map/ppermute | solution.py:58
  247.6 5.7 %collective-permute-done.30 = bf16[1280,128]{1,0:T(8,128)(2,1)S(1)} collective-permute-done((bf16[1280,128]{1,0:T(8,128)(2,1)S(1)}, bf16[1280,128]{1,0:T(8,128)(2,1)S(1)}, u32[]{:S(2)}, u32[]{:S(2)}) %collective-permute-start.30) | collective-permute-done | bytes 327712 | tf_op jit(solution)/shard_map/ppermute | solution.py:58
  254.0 2.1 shard_map.155
  257.5 3.2 %reshape.129 = bf16[1,32,6400]{2,1,0:T(8,128)(2,1)} reshape(bf16[4,8,4,40,40]{4,3,2,1,0:T(8,128)(2,1)S(1)} %copy.32) | data formatting | bytes 819200 | tf_op jit(solution)/shard_map/reshape | solution.py:432
  260.7 1.9 fusion.20
  (176 shorter events, 62.8 us)
Async XLA Ops:
  0.6 22.9 %collective-permute-start = (bf16[1280,128]{1,0:T(8,128)(2,1)}, bf16[1280,128]{1,0:T(8,128)(2,1)}, u32[]{:S(2)}, u32[]{:S(2)}) collective-permute-start(bf16[1280,128]{1,0:T(8,128)(2,1)} %bitcast.231), channel_id=1, source_target_pairs={{0,1},{1,0},{2,3},{3,2},{4,5},{5,4},{6,7},{7,6},{8,9},{9,8},{10,11... | collective-permute-start | bytes 983048 | tf_op jit(solution)/shard_map/ppermute | solution.py:41
  3.6 28.6 %collective-permute-start.2 = (bf16[1280,128]{1,0:T(8,128)(2,1)}, bf16[1280,128]{1,0:T(8,128)(2,1)}, u32[]{:S(2)}, u32[]{:S(2)}) collective-permute-start(bf16[1280,128]{1,0:T(8,128)(2,1)} %bitcast.232), channel_id=1, source_target_pairs={{0,3},{1,2},{2,1},{3,0},{4,7},{5,6},{6,5},{7,4},{8,11},{9,10},{10,... | collective-permute-start | bytes 983048 | tf_op jit(solution)/shard_map/ppermute | solution.py:41
  5.1 25.4 %collective-permute-start.1 = (bf16[1280,128]{1,0:T(8,128)(2,1)}, bf16[1280,128]{1,0:T(8,128)(2,1)}, u32[]{:S(2)}, u32[]{:S(2)}) collective-permute-start(bf16[1280,128]{1,0:T(8,128)(2,1)} %bitcast.233), channel_id=1, source_target_pairs={{0,2},{1,3},{2,0},{3,1},{4,6},{5,7},{6,4},{7,5},{8,10},{9,11},{10,... | collective-permute-start | bytes 983048 | tf_op jit(solution)/shard_map/ppermute | solution.py:41
  12.5 4.5 %copy-start.31 = (bf16[1,2,1280,128]{3,2,1,0:T(8,128)(2,1)S(1)}, bf16[1,2,1280,128]{3,2,1,0:T(8,128)(2,1)}, u32[]{:S(2)}) copy-start(bf16[1,2,1280,128]{3,2,1,0:T(8,128)(2,1)} %param.11) | copy-start | bytes 1966084
  12.5 24.6 %all-to-all-start = ((bf16[4,4,3,40,320]{4,3,2,1,0:T(8,128)(2,1)}), bf16[4,4,3,40,320]{4,3,2,1,0:T(8,128)(2,1)S(1)}, u32[]{:S(2)}, u32[]{:S(2)}) async-start(bf16[4,4,3,40,320]{4,3,2,1,0:T(8,128)(2,1)} %shard_map.136), calls=%async_computation | async-start | bytes 2949120 | tf_op jit(solution)/shard_map/all_to_all | solution.py:271
  23.5 17.0 %copy-start.26 = (bf16[1,1280,128]{2,1,0:T(8,128)(2,1)S(1)}, bf16[1,1280,128]{2,1,0:T(8,128)(2,1)}, u32[]{:S(2)}) copy-start(bf16[1,1280,128]{2,1,0:T(8,128)(2,1)} %param.12) | copy-start | bytes 983044
  37.0 17.2 %collective-permute-start.8 = (bf16[1280,128]{1,0:T(8,128)(2,1)}, bf16[1280,128]{1,0:T(8,128)(2,1)S(1)}, u32[]{:S(2)}, u32[]{:S(2)}) collective-permute-start(bf16[1280,128]{1,0:T(8,128)(2,1)} %get-tuple-element.61), channel_id=1, source_target_pairs={{0,3},{1,2},{2,1},{3,0},{4,7},{5,6},{6,5},{7,4},{8,11},{9,10},{10,... | collective-permute-start | bytes 983048 | tf_op jit(solution)/shard_map/ppermute | solution.py:41
  38.5 17.4 %collective-permute-start.7 = (bf16[1280,128]{1,0:T(8,128)(2,1)}, bf16[1280,128]{1,0:T(8,128)(2,1)S(1)}, u32[]{:S(2)}, u32[]{:S(2)}) collective-permute-start(bf16[1280,128]{1,0:T(8,128)(2,1)} %get-tuple-element.61), channel_id=1, source_target_pairs={{0,2},{1,3},{2,0},{3,1},{4,6},{5,7},{6,4},{7,5},{8,10},{9,11},{10,... | collective-permute-start | bytes 983048 | tf_op jit(solution)/shard_map/ppermute | solution.py:41
  40.0 17.3 %collective-permute-start.6 = (bf16[1280,128]{1,0:T(8,128)(2,1)}, bf16[1280,128]{1,0:T(8,128)(2,1)S(1)}, u32[]{:S(2)}, u32[]{:S(2)}) collective-permute-start(bf16[1280,128]{1,0:T(8,128)(2,1)} %get-tuple-element.61), channel_id=1, source_target_pairs={{0,1},{1,0},{2,3},{3,2},{4,5},{5,4},{6,7},{7,6},{8,9},{9,8},{10,11... | collective-permute-start | bytes 983048 | tf_op jit(solution)/shard_map/ppermute | solution.py:41
  40.5 31.5 %collective-permute-start.15 = (bf16[1280,128]{1,0:T(8,128)(2,1)S(1)}, bf16[1280,128]{1,0:T(8,128)(2,1)S(1)}, u32[]{:S(2)}, u32[]{:S(2)}) collective-permute-start(bf16[1280,128]{1,0:T(8,128)(2,1)S(1)} %bitcast.234), channel_id=1, source_target_pairs={{0,3},{1,2},{2,1},{3,0},{4,7},{5,6},{6,5},{7,4},{8,11},{9,10},{10,... | collective-permute-start | bytes 983048 | tf_op jit(solution)/shard_map/ppermute | solution.py:41
  42.0 29.5 %collective-permute-start.14 = (bf16[1280,128]{1,0:T(8,128)(2,1)S(1)}, bf16[1280,128]{1,0:T(8,128)(2,1)S(1)}, u32[]{:S(2)}, u32[]{:S(2)}) collective-permute-start(bf16[1280,128]{1,0:T(8,128)(2,1)S(1)} %bitcast.235), channel_id=1, source_target_pairs={{0,2},{1,3},{2,0},{3,1},{4,6},{5,7},{6,4},{7,5},{8,10},{9,11},{10,... | collective-permute-start | bytes 983048 | tf_op jit(solution)/shard_map/ppermute | solution.py:41
  54.2 7.6 %copy-start.28 = (bf16[1280,128]{1,0:T(8,128)(2,1)S(1)}, bf16[1280,128]{1,0:T(8,128)(2,1)}, u32[]{:S(2)}) copy-start(bf16[1280,128]{1,0:T(8,128)(2,1)} %get-tuple-element.61) | copy-start | bytes 983044
  54.2 14.6 %collective-permute-start.13 = (bf16[1280,128]{1,0:T(8,128)(2,1)S(1)}, bf16[1280,128]{1,0:T(8,128)(2,1)S(1)}, u32[]{:S(2)}, u32[]{:S(2)}) collective-permute-start(bf16[1280,128]{1,0:T(8,128)(2,1)S(1)} %bitcast.237), channel_id=1, source_target_pairs={{0,1},{1,0},{2,3},{3,2},{4,5},{5,4},{6,7},{7,6},{8,9},{9,8},{10,11... | collective-permute-start | bytes 983048 | tf_op jit(solution)/shard_map/ppermute | solution.py:41
  55.9 66.7 %collective-permute-start.21 = (bf16[1280,128]{1,0:T(8,128)(2,1)S(1)}, bf16[1280,128]{1,0:T(8,128)(2,1)S(1)}, u32[]{:S(2)}, u32[]{:S(2)}) collective-permute-start(bf16[1280,128]{1,0:T(8,128)(2,1)S(1)} %copy-done.27), channel_id=1, source_target_pairs={{0,3},{1,2},{2,1},{3,0},{4,7},{5,6},{6,5},{7,4},{8,11},{9,10},{10,... | collective-permute-start | bytes 983048 | tf_op jit(solution)/shard_map/ppermute | solution.py:41
  57.3 66.4 %collective-permute-start.20 = (bf16[1280,128]{1,0:T(8,128)(2,1)S(1)}, bf16[1280,128]{1,0:T(8,128)(2,1)S(1)}, u32[]{:S(2)}, u32[]{:S(2)}) collective-permute-start(bf16[1280,128]{1,0:T(8,128)(2,1)S(1)} %copy-done.27), channel_id=1, source_target_pairs={{0,2},{1,3},{2,0},{3,1},{4,6},{5,7},{6,4},{7,5},{8,10},{9,11},{10,... | collective-permute-start | bytes 983048 | tf_op jit(solution)/shard_map/ppermute | solution.py:41
  68.9 15.2 %collective-permute-start.5 = (bf16[1280,128]{1,0:T(8,128)(2,1)S(1)}, bf16[1280,128]{1,0:T(8,128)(2,1)S(1)}, u32[]{:S(2)}, u32[]{:S(2)}) collective-permute-start(bf16[1280,128]{1,0:T(8,128)(2,1)S(1)} %get-tuple-element.125), channel_id=1, source_target_pairs={{0,3},{1,2},{2,1},{3,0},{4,7},{5,6},{6,5},{7,4},{8,11},{9,10},{10,... | collective-permute-start | bytes 983048 | tf_op jit(solution)/shard_map/ppermute | solution.py:58
  71.5 24.3 %collective-permute-start.4 = (bf16[1280,128]{1,0:T(8,128)(2,1)S(1)}, bf16[1280,128]{1,0:T(8,128)(2,1)S(1)}, u32[]{:S(2)}, u32[]{:S(2)}) collective-permute-start(bf16[1280,128]{1,0:T(8,128)(2,1)S(1)} %get-tuple-element.126), channel_id=1, source_target_pairs={{0,2},{1,3},{2,0},{3,1},{4,6},{5,7},{6,4},{7,5},{8,10},{9,11},{10,... | collective-permute-start | bytes 983048 | tf_op jit(solution)/shard_map/ppermute | solution.py:58
  72.1 23.6 %collective-permute-start.3 = (bf16[1280,128]{1,0:T(8,128)(2,1)S(1)}, bf16[1280,128]{1,0:T(8,128)(2,1)S(1)}, u32[]{:S(2)}, u32[]{:S(2)}) collective-permute-start(bf16[1280,128]{1,0:T(8,128)(2,1)S(1)} %get-tuple-element.127), channel_id=1, source_target_pairs={{0,1},{1,0},{2,3},{3,2},{4,5},{5,4},{6,7},{7,6},{8,9},{9,8},{10,11... | collective-permute-start | bytes 983048 | tf_op jit(solution)/shard_map/ppermute | solution.py:58
  80.2 15.6 %copy-start.32 = (bf16[1280,128]{1,0:T(8,128)(2,1)S(1)}, bf16[1280,128]{1,0:T(8,128)(2,1)}, u32[]{:S(2)}) copy-start(bf16[1280,128]{1,0:T(8,128)(2,1)} %param.10) | copy-start | bytes 983044
  84.0 39.7 %collective-permute-start.19 = (bf16[1280,128]{1,0:T(8,128)(2,1)S(1)}, bf16[1280,128]{1,0:T(8,128)(2,1)S(1)}, u32[]{:S(2)}, u32[]{:S(2)}) collective-permute-start(bf16[1280,128]{1,0:T(8,128)(2,1)S(1)} %copy-done.27), channel_id=1, source_target_pairs={{0,1},{1,0},{2,3},{3,2},{4,5},{5,4},{6,7},{7,6},{8,9},{9,8},{10,11... | collective-permute-start | bytes 983048 | tf_op jit(solution)/shard_map/ppermute | solution.py:41
  96.0 56.3 %collective-permute-start.12 = (bf16[1280,128]{1,0:T(8,128)(2,1)S(1)}, bf16[1280,128]{1,0:T(8,128)(2,1)S(1)}, u32[]{:S(2)}, u32[]{:S(2)}) collective-permute-start(bf16[1280,128]{1,0:T(8,128)(2,1)S(1)} %fusion.18), channel_id=1, source_target_pairs={{0,7},{1,6},{2,5},{3,4},{4,11},{5,10},{6,9},{7,8},{8,15},{9,14},{1... | collective-permute-start | bytes 983048 | tf_op jit(solution)/shard_map/ppermute | solution.py:41
  97.1 55.2 %collective-permute-start.11 = (bf16[1280,128]{1,0:T(8,128)(2,1)S(1)}, bf16[1280,128]{1,0:T(8,128)(2,1)S(1)}, u32[]{:S(2)}, u32[]{:S(2)}) collective-permute-start(bf16[1280,128]{1,0:T(8,128)(2,1)S(1)} %fusion.18), channel_id=1, source_target_pairs={{0,6},{1,7},{2,4},{3,5},{4,10},{5,11},{6,8},{7,9},{8,14},{9,15},{1... | collective-permute-start | bytes 983048 | tf_op jit(solution)/shard_map/ppermute | solution.py:41
  101.5 9.3 %copy-start.5 = (bf16[40,128,128]{2,1,0:T(8,128)(2,1)}, bf16[40,128,128]{2,1,0:T(8,128)(2,1)S(1)}, u32[]{:S(2)}) copy-start(bf16[40,128,128]{2,1,0:T(8,128)(2,1)S(1)} %shard_map.140.grad_ref.refs_2_) | copy-start | bytes 3932164
  118.1 4.3 %copy-start.13 = (f32[16,80,320]{2,1,0:T(8,128)}, f32[16,80,320]{2,1,0:T(8,128)S(1)}, u32[]{:S(2)}) copy-start(f32[16,80,320]{2,1,0:T(8,128)S(1)} %shard_map.146) | copy-start | bytes 4915204
  122.6 29.7 %collective-permute-start.10 = (bf16[1280,128]{1,0:T(8,128)(2,1)S(1)}, bf16[1280,128]{1,0:T(8,128)(2,1)S(1)}, u32[]{:S(2)}, u32[]{:S(2)}) collective-permute-start(bf16[1280,128]{1,0:T(8,128)(2,1)S(1)} %fusion.18), channel_id=1, source_target_pairs={{0,5},{1,4},{2,7},{3,6},{4,9},{5,8},{6,11},{7,10},{8,13},{9,12},{1... | collective-permute-start | bytes 983048 | tf_op jit(solution)/shard_map/ppermute | solution.py:41
  123.7 17.1 %collective-permute-start.18 = (bf16[1280,128]{1,0:T(8,128)(2,1)S(1)}, bf16[1280,128]{1,0:T(8,128)(2,1)S(1)}, u32[]{:S(2)}, u32[]{:S(2)}) collective-permute-start(bf16[1280,128]{1,0:T(8,128)(2,1)S(1)} %get-tuple-element.121), channel_id=1, source_target_pairs={{0,3},{1,2},{2,1},{3,0},{4,7},{5,6},{6,5},{7,4},{8,11},{9,10},{10,... | collective-permute-start | bytes 983048 | tf_op jit(solution)/shard_map/ppermute | solution.py:58
  125.1 17.4 %collective-permute-start.17 = (bf16[1280,128]{1,0:T(8,128)(2,1)S(1)}, bf16[1280,128]{1,0:T(8,128)(2,1)S(1)}, u32[]{:S(2)}, u32[]{:S(2)}) collective-permute-start(bf16[1280,128]{1,0:T(8,128)(2,1)S(1)} %get-tuple-element.122), channel_id=1, source_target_pairs={{0,2},{1,3},{2,0},{3,1},{4,6},{5,7},{6,4},{7,5},{8,10},{9,11},{10,... | collective-permute-start | bytes 983048 | tf_op jit(solution)/shard_map/ppermute | solution.py:58
  133.5 13.0 %copy-start.11 = (bf16[40,128,128]{2,1,0:T(8,128)(2,1)}, bf16[40,128,128]{2,1,0:T(8,128)(2,1)S(1)}, u32[]{:S(2)}) copy-start(bf16[40,128,128]{2,1,0:T(8,128)(2,1)S(1)} %fusion.3.refs_1_) | copy-start | bytes 3932164
  140.8 11.5 %collective-permute-start.9 = (bf16[1280,128]{1,0:T(8,128)(2,1)S(1)}, bf16[1280,128]{1,0:T(8,128)(2,1)S(1)}, u32[]{:S(2)}, u32[]{:S(2)}) collective-permute-start(bf16[1280,128]{1,0:T(8,128)(2,1)S(1)} %fusion.18), channel_id=1, source_target_pairs={{0,4},{1,5},{2,6},{3,7},{4,8},{5,9},{6,10},{7,11},{8,12},{9,13},{1... | collective-permute-start | bytes 983048 | tf_op jit(solution)/shard_map/ppermute | solution.py:41
  142.6 9.7 %collective-permute-start.16 = (bf16[1280,128]{1,0:T(8,128)(2,1)S(1)}, bf16[1280,128]{1,0:T(8,128)(2,1)S(1)}, u32[]{:S(2)}, u32[]{:S(2)}) collective-permute-start(bf16[1280,128]{1,0:T(8,128)(2,1)S(1)} %get-tuple-element.123), channel_id=1, source_target_pairs={{0,1},{1,0},{2,3},{3,2},{4,5},{5,4},{6,7},{7,6},{8,9},{9,8},{10,11... | collective-permute-start | bytes 983048 | tf_op jit(solution)/shard_map/ppermute | solution.py:58
  146.6 5.8 %copy-start.33 = (bf16[1280,128]{1,0:T(8,128)(2,1)S(1)}, bf16[1280,128]{1,0:T(8,128)(2,1)}, u32[]{:S(2)}) copy-start(bf16[1280,128]{1,0:T(8,128)(2,1)} %param.13) | copy-start | bytes 983044
  152.6 14.6 %collective-permute-start.28 = (bf16[1280,128]{1,0:T(8,128)(2,1)S(1)}, bf16[1280,128]{1,0:T(8,128)(2,1)S(1)}, u32[]{:S(2)}, u32[]{:S(2)}) collective-permute-start(bf16[1280,128]{1,0:T(8,128)(2,1)S(1)} %fusion.19), channel_id=1, source_target_pairs={{0,31},{1,30},{2,29},{3,28},{4,3},{5,2},{6,1},{7,0},{8,7},{9,6},{1... | collective-permute-start | bytes 983048 | tf_op jit(solution)/shard_map/ppermute | solution.py:41
  154.6 16.0 %collective-permute-start.27 = (bf16[1280,128]{1,0:T(8,128)(2,1)S(1)}, bf16[1280,128]{1,0:T(8,128)(2,1)S(1)}, u32[]{:S(2)}, u32[]{:S(2)}) collective-permute-start(bf16[1280,128]{1,0:T(8,128)(2,1)S(1)} %fusion.19), channel_id=1, source_target_pairs={{0,30},{1,31},{2,28},{3,29},{4,2},{5,3},{6,0},{7,1},{8,6},{9,7},{1... | collective-permute-start | bytes 983048 | tf_op jit(solution)/shard_map/ppermute | solution.py:41
  155.9 15.6 %collective-permute-start.26 = (bf16[1280,128]{1,0:T(8,128)(2,1)S(1)}, bf16[1280,128]{1,0:T(8,128)(2,1)S(1)}, u32[]{:S(2)}, u32[]{:S(2)}) collective-permute-start(bf16[1280,128]{1,0:T(8,128)(2,1)S(1)} %fusion.19), channel_id=1, source_target_pairs={{0,29},{1,28},{2,31},{3,30},{4,1},{5,0},{6,3},{7,2},{8,5},{9,4},{1... | collective-permute-start | bytes 983048 | tf_op jit(solution)/shard_map/ppermute | solution.py:41
  156.1 15.4 %collective-permute-start.25 = (bf16[1280,128]{1,0:T(8,128)(2,1)S(1)}, bf16[1280,128]{1,0:T(8,128)(2,1)S(1)}, u32[]{:S(2)}, u32[]{:S(2)}) collective-permute-start(bf16[1280,128]{1,0:T(8,128)(2,1)S(1)} %fusion.19), channel_id=1, source_target_pairs={{0,28},{1,29},{2,30},{3,31},{4,0},{5,1},{6,2},{7,3},{8,4},{9,5},{1... | collective-permute-start | bytes 983048 | tf_op jit(solution)/shard_map/ppermute | solution.py:41
  167.0 4.8 %copy-start.15 = (bf16[16,320,128]{2,1,0:T(8,128)(2,1)}, bf16[16,320,128]{2,1,0:T(8,128)(2,1)S(1)}, u32[]{:S(2)}) copy-start(bf16[16,320,128]{2,1,0:T(8,128)(2,1)S(1)} %shard_map.145) | copy-start | bytes 3932164
  201.5 14.6 %copy-start.12 = (bf16[40,128,128]{2,1,0:T(8,128)(2,1)S(1)}, bf16[40,128,128]{2,1,0:T(8,128)(2,1)}, u32[]{:S(2)}) copy-start(bf16[40,128,128]{2,1,0:T(8,128)(2,1)} %copy-done.11) | copy-start | bytes 3932164
  201.5 52.5 %all-to-all-start.1 = ((bf16[4,4,3,40,320]{4,3,2,1,0:T(8,128)(2,1)}), bf16[4,4,3,40,320]{4,3,2,1,0:T(8,128)(2,1)S(1)}, u32[]{:S(2)}, u32[]{:S(2)}) async-start(bf16[4,4,3,40,320]{4,3,2,1,0:T(8,128)(2,1)} %bitcast.225), calls=%async_computation.1 | async-start | bytes 2949120 | tf_op jit(solution)/shard_map/all_to_all | solution.py:409
  206.1 10.1 %copy-start.10 = (bf16[40,128,128]{2,1,0:T(8,128)(2,1)S(1)}, bf16[40,128,128]{2,1,0:T(8,128)(2,1)}, u32[]{:S(2)}) copy-start(bf16[40,128,128]{2,1,0:T(8,128)(2,1)} %copy-done.9) | copy-start | bytes 3932164
  207.4 25.5 %collective-permute-start.22 = (bf16[1280,128]{1,0:T(8,128)(2,1)S(1)}, bf16[1280,128]{1,0:T(8,128)(2,1)S(1)}, u32[]{:S(2)}, u32[]{:S(2)}) collective-permute-start(bf16[1280,128]{1,0:T(8,128)(2,1)S(1)} %get-tuple-element.118), channel_id=1, source_target_pairs={{0,1},{1,0},{2,3},{3,2},{4,5},{5,4},{6,7},{7,6},{8,9},{9,8},{10,11... | collective-permute-start | bytes 983048 | tf_op jit(solution)/shard_map/ppermute | solution.py:58
  209.8 30.9 %collective-permute-start.24 = (bf16[1280,128]{1,0:T(8,128)(2,1)S(1)}, bf16[1280,128]{1,0:T(8,128)(2,1)S(1)}, u32[]{:S(2)}, u32[]{:S(2)}) collective-permute-start(bf16[1280,128]{1,0:T(8,128)(2,1)S(1)} %get-tuple-element.119), channel_id=1, source_target_pairs={{0,3},{1,2},{2,1},{3,0},{4,7},{5,6},{6,5},{7,4},{8,11},{9,10},{10,... | collective-permute-start | bytes 983048 | tf_op jit(solution)/shard_map/ppermute | solution.py:58
  211.1 5.0 %copy-start.6 = (bf16[40,128,128]{2,1,0:T(8,128)(2,1)S(1)}, bf16[40,128,128]{2,1,0:T(8,128)(2,1)}, u32[]{:S(2)}) copy-start(bf16[40,128,128]{2,1,0:T(8,128)(2,1)} %copy-done.5) | copy-start | bytes 3932164
  211.1 5.0 %copy-start.8 = (bf16[40,128,128]{2,1,0:T(8,128)(2,1)S(1)}, bf16[40,128,128]{2,1,0:T(8,128)(2,1)}, u32[]{:S(2)}) copy-start(bf16[40,128,128]{2,1,0:T(8,128)(2,1)} %copy-done.7) | copy-start | bytes 3932164
  211.1 29.5 %collective-permute-start.23 = (bf16[1280,128]{1,0:T(8,128)(2,1)S(1)}, bf16[1280,128]{1,0:T(8,128)(2,1)S(1)}, u32[]{:S(2)}, u32[]{:S(2)}) collective-permute-start(bf16[1280,128]{1,0:T(8,128)(2,1)S(1)} %get-tuple-element.120), channel_id=1, source_target_pairs={{0,2},{1,3},{2,0},{3,1},{4,6},{5,7},{6,4},{7,5},{8,10},{9,11},{10,... | collective-permute-start | bytes 983048 | tf_op jit(solution)/shard_map/ppermute | solution.py:58
  212.8 34.8 %collective-permute-start.31 = (bf16[1280,128]{1,0:T(8,128)(2,1)S(1)}, bf16[1280,128]{1,0:T(8,128)(2,1)S(1)}, u32[]{:S(2)}, u32[]{:S(2)}) collective-permute-start(bf16[1280,128]{1,0:T(8,128)(2,1)S(1)} %get-tuple-element.114), channel_id=1, source_target_pairs={{0,3},{1,2},{2,1},{3,0},{4,7},{5,6},{6,5},{7,4},{8,11},{9,10},{10,... | collective-permute-start | bytes 983048 | tf_op jit(solution)/shard_map/ppermute | solution.py:58
  215.3 37.9 %collective-permute-start.30 = (bf16[1280,128]{1,0:T(8,128)(2,1)S(1)}, bf16[1280,128]{1,0:T(8,128)(2,1)S(1)}, u32[]{:S(2)}, u32[]{:S(2)}) collective-permute-start(bf16[1280,128]{1,0:T(8,128)(2,1)S(1)} %get-tuple-element.115), channel_id=1, source_target_pairs={{0,2},{1,3},{2,0},{3,1},{4,6},{5,7},{6,4},{7,5},{8,10},{9,11},{10,... | collective-permute-start | bytes 983048 | tf_op jit(solution)/shard_map/ppermute | solution.py:58
  232.9 21.1 %collective-permute-start.29 = (bf16[1280,128]{1,0:T(8,128)(2,1)S(1)}, bf16[1280,128]{1,0:T(8,128)(2,1)}, u32[]{:S(2)}, u32[]{:S(2)}) collective-permute-start(bf16[1280,128]{1,0:T(8,128)(2,1)S(1)} %get-tuple-element.116), channel_id=1, source_target_pairs={{0,1},{1,0},{2,3},{3,2},{4,5},{5,4},{6,7},{7,6},{8,9},{9,8},{10,11... | collective-permute-start | bytes 983048 | tf_op jit(solution)/shard_map/ppermute | solution.py:58
  247.6 5.7 %copy-start.34 = (bf16[1280,128]{1,0:T(8,128)(2,1)}, bf16[1280,128]{1,0:T(8,128)(2,1)S(1)}, u32[]{:S(2)}) copy-start(bf16[1280,128]{1,0:T(8,128)(2,1)S(1)} %collective-permute-done.31) | copy-start | bytes 983044
  (24 other events, 51.2 us)
